TPU v7x, 256 devices: a whole 4x4x8 slice. The times are simulated.
256 devices in a mesh: lat: 4 (over x_hi, core), lon: 8 (over x_lo, y), lev: 8 (over z).
Axes of the slice: x: 4 (x_hi: 2, x_lo: 2; x = x_hi * 2 + x_lo), y: 4, z: 8, core: 2. Of those that a mesh axis runs over, the one named last changes fastest.
Arguments:
- target: bfloat16 [4, 768, 64, 1024], P(None, 'lev', 'lat', 'lon'), may hold values from -6 to 6
- hidden: bfloat16 [256, 64, 1024], P(None, 'lat', 'lon'), may hold values from -6 to 6
- weight: bfloat16 [16, 768, 256], P(None, 'lev'), may hold values from -0.1875 to 0.1875
- bias: float32 [768], P('lev'), may hold values from -3 to 3
- gamma: float32 [256, 256], replicated, may hold values from 0 to 0.02
- beta: float32 [256], replicated, may hold values from 0.5 to 2
Outputs:
- grad_hidden: float32 [256, 64, 1024], P(None, 'lat', 'lon')
- grad_weight: float32 [16, 768, 256], P(None, 'lev')
- grad_bias: float32 [768], P('lev')
- grad_gamma: float32 [256, 256], replicated
- grad_beta: float32 [256], replicated
All inputs are finite; a program needn't handle non-finite values.
Results may differ from a plain program's by a relative error of at most 0.0021.
Values may be sent and summed in bfloat16 or wider, within the bound.
A program may use at most 128 MiB of HBM per device.

v0:
```python
import math

import jax
import jax.numpy as jnp
from jax import lax
from jax.sharding import PartitionSpec as P


def extended(array, sides, width, wrap):
    for axis, dim in sides:
        size, length = (lax.axis_size(axis), array.shape[dim])
        up = [(i, (i + 1) % size) for i in range(size if wrap else size - 1)]
        down = [(j, i) for i, j in up]
        last = lax.slice_in_dim(array, length - width, length, axis=dim)
        initial = lax.slice_in_dim(array, 0, width, axis=dim)
        before = lax.ppermute(last, axis, up)
        after = lax.ppermute(initial, axis, down)
        array = jnp.concatenate([before, array, after], axis=dim)
    return array


def window(field, drow, dcol, rows, cols):
    return field[:, 1 + drow : 1 + drow + rows, 1 + dcol : 1 + dcol + cols]


def mixing_back(grad_u, values, root, gamma):
    width_n = values.shape[0]
    flat_grad = grad_u.reshape(width_n, -1)
    flat_values = values.reshape(width_n, -1)
    flat_root = root.reshape(width_n, -1)
    mixing = flat_grad * flat_values / (2.0 * flat_root)
    grad_values = flat_grad * flat_root + 2.0 * flat_values * jnp.dot(
        gamma.T, mixing, precision=lax.Precision.HIGHEST
    )
    gamma_part = jnp.dot(mixing, (flat_values * flat_values).T, precision=lax.Precision.HIGHEST)
    beta_part = jnp.sum(mixing, axis=1)
    return (grad_values.reshape(grad_u.shape), gamma_part, beta_part)


def local(target, hidden, weight, bias, gamma, beta):
    width_n, rows, cols = hidden.shape
    chans = weight.shape[1]
    cells = rows * cols
    total_rows = rows * lax.axis_size("lat")
    total_cells = total_rows * cols * lax.axis_size("lon")
    values = hidden.astype(jnp.float32)
    squares = (values * values).reshape(width_n, cells)
    root = jnp.sqrt(beta[:, None] + jnp.dot(gamma, squares, precision=lax.Precision.HIGHEST))
    inverse = (
        (values.reshape(width_n, cells) * root).astype(jnp.bfloat16).reshape(width_n, rows, cols)
    )
    widened = extended(inverse, (("lon", 2),), 1, True)
    padded = extended(widened, (("lat", 1),), 1, False)
    row_index = (jnp.arange(rows) + lax.axis_index("lat") * rows).astype(jnp.float32)
    bias_sum = jnp.zeros((chans,), jnp.float32)
    residuals = []
    weight_parts = []
    for phase in range(4):
        prow, pcol = (phase // 2, phase % 2)
        moved = jnp.stack(
            [
                window(padded, prow - 1 + tap // 2, pcol - 1 + tap % 2, rows, cols).reshape(
                    width_n, cells
                )
                for tap in range(4)
            ],
            axis=0,
        )
        kernel = weight[4 * phase : 4 * phase + 4]
        recon = (
            lax.dot_general(
                kernel, moved, (((0, 2), (0, 1)), ((), ())), preferred_element_type=jnp.float32
            )
            + bias[:, None]
        )
        area = jnp.cos(math.pi * ((2.0 * row_index + prow + 0.5) / (2.0 * total_rows) - 0.5))
        area_cells = jnp.broadcast_to(area[:, None], (rows, cols)).reshape(cells)
        diff = (recon - target[phase].reshape(chans, cells).astype(jnp.float32)) * area_cells[
            None, :
        ]
        grad_recon = diff.astype(jnp.bfloat16)
        bias_sum = bias_sum + jnp.sum(diff, axis=1)
        weight_parts.append(
            jnp.einsum("tnk,ck->tcn", moved, grad_recon, preferred_element_type=jnp.float32)
        )
        residuals.append(grad_recon.reshape(chans, rows, cols))
    residual = jnp.stack(residuals, axis=0)
    residual_wide = extended(residual, (("lon", 3),), 1, True)
    residual_pad = extended(residual_wide, (("lat", 2),), 1, False)
    pieces = []
    for phase in range(4):
        prow, pcol = (phase // 2, phase % 2)
        for tap in range(4):
            drow, dcol = (prow - 1 + tap // 2, pcol - 1 + tap % 2)
            pieces.append(
                window(residual_pad[phase], -drow, -dcol, rows, cols).reshape(chans, cells)
            )
    stacked = jnp.concatenate(pieces, axis=0)
    kernel_flat = weight.reshape(-1, width_n)
    grad_part = lax.dot_general(
        kernel_flat, stacked, (((0,), (0,)), ((), ())), preferred_element_type=jnp.float32
    ).reshape(width_n, rows, cols)
    grad_weight, grad_bias = lax.psum(
        (jnp.concatenate(weight_parts, axis=0), bias_sum), ("lat", "lon")
    )
    root_field = root.reshape(width_n, rows, cols)
    grad_u = lax.psum(grad_part, "lev")
    grad_hidden, gamma_part, beta_part = mixing_back(grad_u, values, root_field, gamma)
    grad_gamma, grad_beta = lax.psum((gamma_part, beta_part), ("lat", "lon"))
    return (
        grad_hidden,
        grad_weight / total_cells,
        grad_bias / total_cells,
        grad_gamma / total_cells,
        grad_beta / total_cells,
    )


def solution(mesh):
    return jax.shard_map(
        local,
        mesh=mesh,
        in_specs=(
            P(None, "lev", "lat", "lon"),
            P(None, "lat", "lon"),
            P(None, "lev", None),
            P("lev"),
            P(),
            P(),
        ),
        out_specs=(P(None, "lat", "lon"), P(None, "lev", None), P("lev"), P(), P()),
        check_vma=False,
    )
```

profile of v0, /device:TPU:6, one launch (start us, length us, event | category | flops | bytes accessed | tf_op | source)
XLA Modules:
  0.0 384.2 jit_solution(15616898500907696478)
XLA Ops:
  7.2 1.9 copy.35
  10.5 5.3 %fusion.22 = (bf16[256,2048]{0,1:T(8,128)(2,1)S(1)}, f32[256,2048]{0,1:T(8,128)}) fusion(f32[256,16,128]{0,2,1:T(8,128)S(1)} %copy.35, f32[256,256]{1,0:T(8,128)S(1)} %copy-done, f32[32,8,16,128]{3,2,1,0:T(8,128)S(1)} %bitcast.234, f32[256]{0:T(256)S(1)} %copy-done.44), kind=kOutput, calls=%fused_computation.38 | convolution fusion | flops 1612185600 | bytes 7603200 | tf_op jit(solution)/shard_map/dot_general | solution.py:48
  17.5 2.6 collective-permute-start.1
  20.3 2.8 slice_convert_fusion.3
  23.1 1.9 collective-permute-start.2
  25.1 15.6 %collective-permute-start.3 = (bf16[256,1,130]{0,2,1:T(8,128)(2,1)S(1)}, bf16[256,1,130]{0,2,1:T(8,128)(2,1)S(1)}, u32[]{:S(2)}, u32[]{:S(2)}) collective-permute-start(bf16[256,1,130]{0,2,1:T(8,128)(2,1)S(1)} %get-tuple-element.51), channel_id=1, source_target_pairs={{64,0},{128,64},{192,128},{65,1},{129,65},{193,129},{66,2},{130,66... | collective-permute-start | bytes 199688 | tf_op jit(solution)/shard_map/ppermute | solution.py:17
  49.0 2.4 copy.41
  51.4 1.9 copy.75
  53.2 2.4 copy.40
  55.6 3.3 fusion.47
  65.1 2.4 copy.42
  67.5 1.8 copy.81
  69.4 2.4 copy.43
  72.8 4.1 %collective-permute-start.5 = (bf16[4,96,16,1]{1,2,3,0:T(8,128)(2,1)S(1)}, bf16[4,96,16,1]{1,2,3,0:T(8,128)(2,1)S(1)}, u32[]{:S(2)}, u32[]{:S(2)}) collective-permute-start(bf16[4,96,16,1]{1,2,3,0:T(8,128)(2,1)S(1)} %get-tuple-element.37), channel_id=1, source_target_pairs={{8,0},{16,8},{24,16},{32,24},{40,32},{48,40},{56,48},{0,56},{9,1},... | collective-permute-start | bytes 36872 | tf_op jit(solution)/shard_map/ppermute | solution.py:17
  78.6 2.6 pad_maximum_fusion.22
  81.3 1.9 collective-permute-start.6
  83.2 5.1 %collective-permute-start.7 = (bf16[4,96,1,130]{1,2,3,0:T(2,128)(2,1)S(1)}, bf16[4,96,1,130]{1,2,3,0:T(2,128)(2,1)S(1)}, u32[]{:S(2)}, u32[]{:S(2)}) collective-permute-start(bf16[4,96,1,130]{1,2,3,0:T(2,128)(2,1)S(1)} %get-tuple-element.31), channel_id=1, source_target_pairs={{64,0},{128,64},{192,128},{65,1},{129,65},{193,129},{66,2},{130,66... | collective-permute-start | bytes 299528 | tf_op jit(solution)/shard_map/ppermute | solution.py:17
  88.4 2.2 collective-permute-done.6
  92.3 4.0 %pad_maximum_fusion.4 = bf16[4,96,18,130]{1,2,3,0:T(8,128)(2,1)S(1)} fusion(bf16[4,96,1,130]{1,2,3,0:T(2,128)(2,1)S(1)} %collective-permute-done.7, bf16[4,96,16,1]{1,2,3,0:T(8,128)(2,1)S(1)} %collective-permute-done.5, bf16[1,96,16,128]{1,2,3,0:T(8,128)(2,1)S(1)} %copy-done.6, bf16[1,96,16,128]{1,2,3,0:T(8,128)(2,1)S(1)} %copy-done.5, ...), kind=kLoop, calls=%fused_computation.4 | loop fusion | flops 14376960 | bytes 3594240 | tf_op jit(solution)/shard_map/concatenate | solution.py:18
  99.4 2.4 copy.59
  101.8 2.4 copy.58
  104.2 2.4 copy.57
  106.6 2.4 copy.56
  109.0 3.5 fusion.50
  112.6 2.4 copy.55
  115.0 2.4 copy.54
  117.4 2.4 copy.53
  119.9 2.4 copy.52
  122.3 4.2 %fusion.51 = (bf16[96,16,128]{0,1,2:T(8,128)(2,1)}, bf16[96,16,128]{0,1,2:T(8,128)(2,1)}, bf16[96,16,128]{0,1,2:T(8,128)(2,1)}, bf16[96,16,128]{0,1,2:T(8,128)(2,1)}) fusion(bf16[96,18,130]{0,1,2:T(8,128)(2,1)} %get-tuple-element.28), kind=kLoop, calls=%fused_computation.127 | loop fusion | bytes 3145728 | tf_op jit(solution)/shard_map/slice | solution.py:23
  126.5 2.4 copy.51
  128.9 2.4 copy.50
  131.3 2.4 copy.49
  133.7 2.4 copy.48
  136.1 4.1 %fusion.52 = (bf16[96,16,128]{0,1,2:T(8,128)(2,1)}, bf16[96,16,128]{0,1,2:T(8,128)(2,1)}, bf16[96,16,128]{0,1,2:T(8,128)(2,1)}, bf16[96,16,128]{0,1,2:T(8,128)(2,1)}) fusion(bf16[96,18,130]{0,1,2:T(8,128)(2,1)} %get-tuple-element.29), kind=kLoop, calls=%fused_computation.128 | loop fusion | bytes 3145728 | tf_op jit(solution)/shard_map/slice | solution.py:23
  140.3 2.4 copy.47
  142.7 2.6 copy.46
  145.3 2.4 copy.45
  147.7 2.4 copy.44
  157.1 3.3 convolution_bitcast_fusion
  160.5 3.1 convolution_bitcast_fusion.9
  169.3 77.2 %all-reduce.5.cloned.1.call-done = f32[256,2048]{0,1:T(8,128)} async-done(((f32[256,2048]{0,1:T(8,128)}), f32[256,2048]{0,1:T(8,128)}) %all-reduce.5.cloned.1.call-update) | async-done | bytes 2097168 | tf_op jit(solution)/shard_map/psum | solution.py:107
  246.5 4.3 %bitcast_multiply_fusion = (f32[256,2048]{0,1:T(8,128)S(1)}, f32[256,2048]{0,1:T(8,128)}, f32[256]{0:T(256)S(1)}, f32[256,2048]{0,1:T(8,128)S(1)}) fusion(f32[256,16,128]{0,2,1:T(8,128)S(1)} %copy.35, f32[256,2048]{0,1:T(8,128)} %get-tuple-element.81, f32[256,2048]{0,1:T(8,128)} %all-reduce.5.cloned.1.call-done), kind=kLoop, calls=%fused_computation.34 | loop fusion | flops 3145472 | bytes 12583936 | tf_op jit(solution)/shard_map/mul | solution.py:35
  252.2 4.3 %fusion.57 = f32[256,256]{1,0:T(8,128)} fusion(f32[256,2048]{0,1:T(8,128)S(1)} %get-tuple-element.35, f32[256,2048]{0,1:T(8,128)S(1)} %get-tuple-element.32), kind=kOutput, calls=%fused_computation.133 | convolution fusion | flops 1610612736 | bytes 4456448 | tf_op jit(solution)/shard_map/dot_general | solution.py:35
  256.5 6.1 %fusion.1 = f32[256,2048]{0,1:T(8,128)} fusion(f32[256,2048]{0,1:T(8,128)} %get-tuple-element.33, f32[256,2048]{0,1:T(8,128)} %copy-done.1, f32[256,256]{1,0:T(8,128)S(1)} %copy-done, f32[256,2048]{0,1:T(8,128)} %all-reduce.5.cloned.1.call-done, f32[256,2048]{0,1:T(8,128)S(1)} %copy-done.2), kind=kOutput, calls=%fused_computation.8 | convolution fusion | flops 1612185600 | bytes 10747904 | tf_op jit(solution)/shard_map/dot_general | solution.py:32
  262.5 3.0 copy.64
  265.6 63.1 %all-reduce = (f32[96]{0:T(128)S(1)}, f32[256]{0:T(256)S(1)}) all-reduce(f32[96]{0:T(128)S(1)} %add_add_fusion, f32[256]{0:T(256)S(1)} %get-tuple-element.34), channel_id=1, replica_groups=mesh['lat'=4,'lon'=8,'lev'=8] {'lat','lon'}, use_global_device_ids=true, to_apply=%region_6.0 | all-reduce | flops 352 | bytes 2816 | tf_op jit(solution)/shard_map/psum | solution.py:103
  329.7 43.1 %all-reduce.7.cloned.1.call-done = (f32[16,96,256]{2,1,0:T(8,128)}, f32[256,256]{1,0:T(8,128)}) async-done(((f32[16,96,256]{2,1,0:T(8,128)}, f32[256,256]{1,0:T(8,128)}), (f32[16,96,256]{2,1,0:T(8,128)}, f32[256,256]{1,0:T(8,128)})) %all-reduce.7.cloned.1.call-update) | async-done | bytes 1835024 | tf_op jit(solution)/shard_map/psum | solution.py:103
  372.8 2.7 broadcast_multiply_fusion
  (156 shorter events, 41.8 us)
Async XLA Ops:
  7.2 3.3 copy-start
  7.2 3.3 copy-start.44
  7.2 239.3 %all-reduce.5.cloned.1.call-start = ((), (), s32[]{:S(2)}) async-start(), calls=%async_computation | async-start | bytes 4194304 | tf_op jit(solution)/shard_map/psum | solution.py:107
  15.9 7.2 %collective-permute-start = (bf16[256,16,1]{0,2,1:T(2,128)(2,1)S(1)}, bf16[256,16,1]{0,2,1:T(2,128)(2,1)S(1)}, u32[]{:S(2)}, u32[]{:S(2)}) collective-permute-start(bf16[256,16,1]{0,2,1:T(2,128)(2,1)S(1)} %get-tuple-element.54), channel_id=1, source_target_pairs={{0,8},{8,16},{16,24},{24,32},{32,40},{40,48},{48,56},{56,0},{1,9},... | collective-permute-start | bytes 24584 | tf_op jit(solution)/shard_map/ppermute | solution.py:16
  17.5 5.6 %collective-permute-start.1 = (bf16[256,16,1]{0,2,1:T(2,128)(2,1)S(1)}, bf16[256,16,1]{0,2,1:T(2,128)(2,1)S(1)}, u32[]{:S(2)}, u32[]{:S(2)}) collective-permute-start(bf16[256,16,1]{0,2,1:T(2,128)(2,1)S(1)} %get-tuple-element.55), channel_id=1, source_target_pairs={{8,0},{16,8},{24,16},{32,24},{40,32},{48,40},{56,48},{0,56},{9,1},... | collective-permute-start | bytes 24584 | tf_op jit(solution)/shard_map/ppermute | solution.py:17
  23.1 18.2 %collective-permute-start.2 = (bf16[256,1,130]{0,2,1:T(8,128)(2,1)S(1)}, bf16[256,1,130]{0,2,1:T(8,128)(2,1)S(1)}, u32[]{:S(2)}, u32[]{:S(2)}) collective-permute-start(bf16[256,1,130]{0,2,1:T(8,128)(2,1)S(1)} %get-tuple-element.50), channel_id=1, source_target_pairs={{0,64},{64,128},{128,192},{1,65},{65,129},{129,193},{2,66},{66,130... | collective-permute-start | bytes 199688 | tf_op jit(solution)/shard_map/ppermute | solution.py:16
  25.1 16.3 %collective-permute-start.3 = (bf16[256,1,130]{0,2,1:T(8,128)(2,1)S(1)}, bf16[256,1,130]{0,2,1:T(8,128)(2,1)S(1)}, u32[]{:S(2)}, u32[]{:S(2)}) collective-permute-start(bf16[256,1,130]{0,2,1:T(8,128)(2,1)S(1)} %get-tuple-element.51), channel_id=1, source_target_pairs={{64,0},{128,64},{192,128},{65,1},{129,65},{193,129},{66,2},{130,66... | collective-permute-start | bytes 199688 | tf_op jit(solution)/shard_map/ppermute | solution.py:17
  41.3 2.4 copy-start.21
  41.3 4.1 %copy-start.18 = (bf16[256,16,128]{0,2,1:T(8,128)(2,1)}, bf16[256,16,128]{0,2,1:T(8,128)(2,1)S(1)}, u32[]{:S(2)}) copy-start(bf16[256,16,128]{0,2,1:T(8,128)(2,1)S(1)} %get-tuple-element.53) | copy-start | bytes 3145732
  41.3 2.4 copy-start.45
  41.4 2.4 copy-start.48
  47.0 2.0 copy-start.38
  55.6 3.4 copy-start.22
  55.6 3.4 copy-start.36
  55.6 3.4 copy-start.46
  59.0 1.7 copy-start.29
  59.0 1.7 copy-start.31
  59.0 2.0 copy-start.19
  59.0 2.5 copy-start.35
  60.6 2.5 copy-start.42
  63.1 2.0 copy-start.40
  71.8 20.5 %copy-start.3 = (bf16[1,96,16,128]{1,2,3,0:T(8,128)(2,1)S(1)}, bf16[1,96,16,128]{1,2,3,0:T(8,128)(2,1)}, u32[]{:S(2)}) copy-start(bf16[1,96,16,128]{1,2,3,0:T(8,128)(2,1)} %copy.41) | copy-start | bytes 1179652
  71.8 20.5 %copy-start.4 = (bf16[1,96,16,128]{1,2,3,0:T(8,128)(2,1)S(1)}, bf16[1,96,16,128]{1,2,3,0:T(8,128)(2,1)}, u32[]{:S(2)}) copy-start(bf16[1,96,16,128]{1,2,3,0:T(8,128)(2,1)} %copy.40) | copy-start | bytes 1179652
  71.8 20.5 %copy-start.5 = (bf16[1,96,16,128]{1,2,3,0:T(8,128)(2,1)S(1)}, bf16[1,96,16,128]{1,2,3,0:T(8,128)(2,1)}, u32[]{:S(2)}) copy-start(bf16[1,96,16,128]{1,2,3,0:T(8,128)(2,1)} %copy.42) | copy-start | bytes 1179652
  71.8 20.5 %copy-start.6 = (bf16[1,96,16,128]{1,2,3,0:T(8,128)(2,1)S(1)}, bf16[1,96,16,128]{1,2,3,0:T(8,128)(2,1)}, u32[]{:S(2)}) copy-start(bf16[1,96,16,128]{1,2,3,0:T(8,128)(2,1)} %copy.43) | copy-start | bytes 1179652
  72.7 5.9 %collective-permute-start.4 = (bf16[4,96,16,1]{1,2,3,0:T(8,128)(2,1)S(1)}, bf16[4,96,16,1]{1,2,3,0:T(8,128)(2,1)S(1)}, u32[]{:S(2)}, u32[]{:S(2)}) collective-permute-start(bf16[4,96,16,1]{1,2,3,0:T(8,128)(2,1)S(1)} %get-tuple-element.36), channel_id=1, source_target_pairs={{0,8},{8,16},{16,24},{24,32},{32,40},{40,48},{48,56},{56,0},{1,9},... | collective-permute-start | bytes 36872 | tf_op jit(solution)/shard_map/ppermute | solution.py:16
  72.8 5.8 %collective-permute-start.5 = (bf16[4,96,16,1]{1,2,3,0:T(8,128)(2,1)S(1)}, bf16[4,96,16,1]{1,2,3,0:T(8,128)(2,1)S(1)}, u32[]{:S(2)}, u32[]{:S(2)}) collective-permute-start(bf16[4,96,16,1]{1,2,3,0:T(8,128)(2,1)S(1)} %get-tuple-element.37), channel_id=1, source_target_pairs={{8,0},{16,8},{24,16},{32,24},{40,32},{48,40},{56,48},{0,56},{9,1},... | collective-permute-start | bytes 36872 | tf_op jit(solution)/shard_map/ppermute | solution.py:17
  81.3 9.2 %collective-permute-start.6 = (bf16[4,96,1,130]{1,2,3,0:T(2,128)(2,1)S(1)}, bf16[4,96,1,130]{1,2,3,0:T(2,128)(2,1)S(1)}, u32[]{:S(2)}, u32[]{:S(2)}) collective-permute-start(bf16[4,96,1,130]{1,2,3,0:T(2,128)(2,1)S(1)} %get-tuple-element.30), channel_id=1, source_target_pairs={{0,64},{64,128},{128,192},{1,65},{65,129},{129,193},{2,66},{66,130... | collective-permute-start | bytes 299528 | tf_op jit(solution)/shard_map/ppermute | solution.py:16
  83.2 9.1 %collective-permute-start.7 = (bf16[4,96,1,130]{1,2,3,0:T(2,128)(2,1)S(1)}, bf16[4,96,1,130]{1,2,3,0:T(2,128)(2,1)S(1)}, u32[]{:S(2)}, u32[]{:S(2)}) collective-permute-start(bf16[4,96,1,130]{1,2,3,0:T(2,128)(2,1)S(1)} %get-tuple-element.31), channel_id=1, source_target_pairs={{64,0},{128,64},{192,128},{65,1},{129,65},{193,129},{66,2},{130,66... | collective-permute-start | bytes 299528 | tf_op jit(solution)/shard_map/ppermute | solution.py:17
  150.1 5.8 %copy-start.17 = (bf16[96,16,128]{2,1,0:T(8,128)(2,1)S(1)}, bf16[96,16,128]{2,1,0:T(8,128)(2,1)}, u32[]{:S(2)}) copy-start(bf16[96,16,128]{2,1,0:T(8,128)(2,1)} %copy.49) | copy-start | bytes 1179652
  150.1 5.9 %copy-start.16 = (bf16[96,16,128]{2,1,0:T(8,128)(2,1)S(1)}, bf16[96,16,128]{2,1,0:T(8,128)(2,1)}, u32[]{:S(2)}) copy-start(bf16[96,16,128]{2,1,0:T(8,128)(2,1)} %copy.50) | copy-start | bytes 1179652
  150.1 6.0 %copy-start.15 = (bf16[96,16,128]{2,1,0:T(8,128)(2,1)S(1)}, bf16[96,16,128]{2,1,0:T(8,128)(2,1)}, u32[]{:S(2)}) copy-start(bf16[96,16,128]{2,1,0:T(8,128)(2,1)} %copy.51) | copy-start | bytes 1179652
  150.1 6.1 %copy-start.14 = (bf16[96,16,128]{2,1,0:T(8,128)(2,1)S(1)}, bf16[96,16,128]{2,1,0:T(8,128)(2,1)}, u32[]{:S(2)}) copy-start(bf16[96,16,128]{2,1,0:T(8,128)(2,1)} %copy.52) | copy-start | bytes 1179652
  150.1 6.2 %copy-start.13 = (bf16[96,16,128]{2,1,0:T(8,128)(2,1)S(1)}, bf16[96,16,128]{2,1,0:T(8,128)(2,1)}, u32[]{:S(2)}) copy-start(bf16[96,16,128]{2,1,0:T(8,128)(2,1)} %copy.53) | copy-start | bytes 1179652
  150.1 6.3 %copy-start.12 = (bf16[96,16,128]{2,1,0:T(8,128)(2,1)S(1)}, bf16[96,16,128]{2,1,0:T(8,128)(2,1)}, u32[]{:S(2)}) copy-start(bf16[96,16,128]{2,1,0:T(8,128)(2,1)} %copy.54) | copy-start | bytes 1179652
  150.1 6.4 %copy-start.11 = (bf16[96,16,128]{2,1,0:T(8,128)(2,1)S(1)}, bf16[96,16,128]{2,1,0:T(8,128)(2,1)}, u32[]{:S(2)}) copy-start(bf16[96,16,128]{2,1,0:T(8,128)(2,1)} %copy.55) | copy-start | bytes 1179652
  151.4 5.2 %copy-start.10 = (bf16[96,16,128]{2,1,0:T(8,128)(2,1)S(1)}, bf16[96,16,128]{2,1,0:T(8,128)(2,1)}, u32[]{:S(2)}) copy-start(bf16[96,16,128]{2,1,0:T(8,128)(2,1)} %copy.56) | copy-start | bytes 1179652
  152.5 4.2 %copy-start.9 = (bf16[96,16,128]{2,1,0:T(8,128)(2,1)S(1)}, bf16[96,16,128]{2,1,0:T(8,128)(2,1)}, u32[]{:S(2)}) copy-start(bf16[96,16,128]{2,1,0:T(8,128)(2,1)} %copy.57) | copy-start | bytes 1179652
  153.7 3.2 copy-start.8
  154.8 2.1 copy-start.7
  160.4 212.4 %all-reduce.7.cloned.1.call-start = ((), (), s32[]{:S(2)}) async-start(), calls=%async_computation.1 | async-start | bytes 3670016 | tf_op jit(solution)/shard_map/psum | solution.py:103
  160.4 3.1 copy-start.20
  160.4 3.1 copy-start.25
  160.5 3.1 copy-start.27
  160.5 3.2 copy-start.39
  163.7 1.9 copy-start.34
  163.7 2.1 copy-start.43
  250.8 5.7 %copy-start.2 = (f32[256,2048]{0,1:T(8,128)S(1)}, f32[256,2048]{0,1:T(8,128)}, u32[]{:S(2)}) copy-start(f32[256,2048]{0,1:T(8,128)} %get-tuple-element.81) | copy-start | bytes 6291460
  (11 other events, 16.3 us)
Sparse Core Ops, SparseCore 0:
  160.5 85.9 all-reduce.4
  256.6 116.1 all-reduce.6
where the time goes:
time: 391 us; the launch traced here: 384 us
  waiting for transfers between devices  126 us (32%)
  local copies, waits for them, and re-layouts  89 us (23%)
  blocking collectives  63.1 us (16%)
  starting transfers between devices  33.1 us (8%)
  matrix products  30.7 us (8%)
  other arithmetic  27.3 us (7%)
  between operations  15 us (4%)
    psum x1, waiting for transfers between devices, local(): grad_u = lax.psum(grad_part, 'lev')  77.2 us
    psum x1, blocking collectives, local(): lax.psum((jnp.concatenate(weight_parts, axis=0), bias_sum), ('lat', 'lon'))  63.1 us
    slice x22, local copies, waits for them, and re-layouts, window(): return field[:, 1 + drow:1 + drow + rows, 1 + dcol:1 + dcol + cols]  56 us
    psum x1, waiting for transfers between devices, local(): lax.psum((jnp.concatenate(weight_parts, axis=0), bias_sum), ('lat', 'lon'))  43.1 us
    ppermute x4, starting transfers between devices, extended(): after = lax.ppermute(initial, axis, down)  27.5 us
    unnamed x118, local copies, waits for them, and re-layouts  19.5 us
    another operation x4, local copies, waits for them, and re-layouts, local(): residual = jnp.stack(residuals, axis=0)  9.6 us
  transfers between devices with their start and end apart: 10, of which 5 were waited for; matrix products, arithmetic and copies ran while one was open for 5% of the time, Pallas kernels for 0%

commit v1 on v0

v1 whole, which is shorter than its diff:
```python
import functools
import math

import jax
import jax.numpy as jnp
import numpy as np
from jax import lax
from jax.experimental import pallas as pl
from jax.experimental.pallas import tpu as pltpu
from jax.sharding import PartitionSpec as P

F32 = jnp.float32
BF16 = jnp.bfloat16
MESH = pl.DeviceIdType.MESH
LANES = 128


def split(x):
    hi = x.astype(BF16)
    return hi, (x - hi.astype(F32)).astype(BF16)


def dot(a, b):
    return jnp.dot(a, b, preferred_element_type=F32)


def dot_nt(a, b):
    return lax.dot_general(a, b, (((1,), (1,)), ((), ())), preferred_element_type=F32)


def wrap(index, size):
    return lax.rem(index + size, size)


def kernel(
    dims,
    area_ref, hidden_ref, target_ref, weight_ref, bias_ref, gamma_ref, beta_ref,
    gh_out, gw_out, gb_out, gg_out, gbeta_out,
    hid_v, tgt_v, w_v, gamma_v,
    hf, tf, hx, root_s, hr_s, sqh, sql, g3, gt3, wt,
    us, gs, sel, sr,
    hh_send, hh_recv, eu_send, eu_recv, eg_send, eg_recv,
    dw, dwp, rsb, rsr, wg,
    gu, bacc, mh, ml, ext, extp, exts, extr, extz, extg,
    abuf, arecv, agr, gho,
    in_sem, out_sem,
    row_ss, row_rs, eu_ss, eu_rs, grow_ss, grow_rs, eg_ss, eg_rs,
    pw_ss, pw_rs, rb_ss, rb_rs, ab_ss, ab_rs, pg_ss, pg_rs,
    pe_ss, pe_rs, rc_ss, rc_rs, z_ss, z_rs, ac_ss, ac_rs, pc_ss, pc_rs,
    a_ss, a_rs, g_ss, g_rs,
):
    nn, rows, chans, n_lat, n_lon, n_lev, n_y, total_cells = dims
    cells = rows * LANES
    rpad = rows + 2
    lat, lon, lev = lax.axis_index("lat"), lax.axis_index("lon"), lax.axis_index("lev")
    core = lax.rem(lat, 2)
    n_chip = (n_lat // 2) * n_lon
    n_xlo = n_lon // n_y
    chip = lax.div(lat, 2) * n_lon + lon
    half = 16 // 2 * chans // n_chip
    share = nn // 2 // n_chip

    def at_chip(k):
        return (lax.div(k, n_lon) * 2 + core, lax.rem(k, n_lon), lev)

    pair = (lat + 1 - 2 * core, lon, lev)
    north = (wrap(lat - 1, n_lat), lon, lev)
    south = (wrap(lat + 1, n_lat), lon, lev)
    west = (lat, wrap(lon - 1, n_lon), lev)
    east = (lat, wrap(lon + 1, n_lon), lev)
    below = (lat, lon, wrap(lev - 1, n_lev))
    above = (lat, lon, wrap(lev + 1, n_lev))

    def remote(src, dst, ss, rs, device):
        return pltpu.make_async_remote_copy(
            src_ref=src, dst_ref=dst, send_sem=ss, recv_sem=rs,
            device_id=device, device_id_type=MESH,
        )

    def lanes(r, count=1):
        if isinstance(r, int):
            return pl.ds(r * LANES, count * LANES)
        return pl.ds(pl.multiple_of(r * LANES, LANES), count * LANES)

    inputs = [
        pltpu.make_async_copy(s, d, in_sem.at[i])
        for i, (s, d) in enumerate(
            ((hidden_ref, hid_v), (gamma_ref, gamma_v), (target_ref, tgt_v), (weight_ref, w_v))
        )
    ]
    for c in inputs:
        c.start()

    barrier = pltpu.get_barrier_semaphore()

    def greet(device):
        pl.semaphore_signal(barrier, inc=1, device_id=device, device_id_type=MESH)

    greet(pair)
    greet((n_lat - 1 - lat, lon, lev))

    def greet_chip(j, c):
        greet(at_chip(wrap(chip + j, n_chip)))
        return c

    lax.fori_loop(1, n_chip, greet_chip, 0)

    def greet_lev(j, c):
        greet((lat, lon, wrap(lev + j, n_lev)))
        return c

    lax.fori_loop(1, n_lev, greet_lev, 0)

    inputs[0].wait()
    hf[...] = hid_v[...].astype(F32).reshape(nn * rows, LANES)

    def spread(i, c):
        hx[:, lanes(i + 1)] = hf[pl.ds(i, nn, stride=rows), :]
        return c

    lax.fori_loop(0, rows, spread, 0)
    hh_send[0] = hx[:, lanes(1)].astype(BF16)
    hh_send[1] = hx[:, lanes(rows)].astype(BF16)
    pl.semaphore_wait(barrier, 2 + (n_chip - 1) + (n_lev - 1))

    sends = []

    def go(copy):
        copy.start()
        sends.append(copy)
        return copy

    row_copies = [
        go(remote(hh_send.at[0], hh_recv.at[1], row_ss.at[0], row_rs.at[0], north)),
        go(remote(hh_send.at[1], hh_recv.at[0], row_ss.at[1], row_rs.at[1], south)),
    ]

    def make_sel(r, c):
        k = lax.broadcasted_iota(jnp.int32, (LANES, LANES), 0)
        e = lax.broadcasted_iota(jnp.int32, (LANES, LANES), 1)
        hit = ((k == LANES - 1) & (e == r)) | ((k == 0) & (e == 32 + r))
        sel[lanes(r), :] = jnp.where(hit, 1.0, 0.0).astype(BF16)
        ki = lax.broadcasted_iota(jnp.int32, (2 * LANES, 2 * LANES), 0)
        o = lax.broadcasted_iota(jnp.int32, (2 * LANES, 2 * LANES), 1)
        low = ki < LANES
        hit = (
            (low & (o < LANES) & (ki == o - 1))
            | (low & (o >= LANES) & (ki == o - LANES + 1))
            | ((o == 0) & (ki == LANES + r))
            | ((o == 2 * LANES - 1) & (ki == LANES + 32 + r))
        )
        sr[r] = jnp.where(hit, 1.0, 0.0).astype(BF16)
        return c

    lax.fori_loop(0, rpad, make_sel, 0)

    inputs[1].wait()
    gamma = gamma_v[...]
    g_hi, g_lo = split(gamma)
    g3[...] = jnp.concatenate([g_hi, g_lo, g_hi], axis=1)
    g_hi, g_lo = split(gamma.T)
    gt3[...] = jnp.concatenate([g_hi, g_lo, g_hi], axis=1)
    eye = lax.broadcasted_iota(jnp.int32, (nn, nn), 0) == lax.broadcasted_iota(
        jnp.int32, (nn, nn), 1
    )
    beta_col = jnp.sum(jnp.where(eye, beta_ref[...], 0.0), axis=1, keepdims=True)
    eye_c = lax.broadcasted_iota(jnp.int32, (chans, chans), 0) == lax.broadcasted_iota(
        jnp.int32, (chans, chans), 1
    )
    bias_col = jnp.sum(jnp.where(eye_c, bias_ref[...], 0.0), axis=1, keepdims=True)

    def root_of(x):
        s_hi, s_lo = split(x * x)
        total = dot(g3[...], jnp.concatenate([s_hi, s_hi, s_lo], axis=0))
        return jnp.sqrt(beta_col + total), s_hi, s_lo

    def root_tile(t, c):
        at = lanes(2 * t, 2)
        x = hx[:, lanes(2 * t + 1, 2)]
        root, s_hi, s_lo = root_of(x)
        root_s[:, at] = root
        hr_s[:, at] = x * (0.5 / root)
        sqh[:, at] = s_hi
        sql[:, at] = s_lo
        us[nn : 2 * nn, lanes(2 * t + 1, 2)] = (x * root).astype(BF16)
        return c

    lax.fori_loop(0, rows // 2, root_tile, 0)

    for c in row_copies:
        c.wait_recv()
    north_in = jnp.where(lat > 0, 1.0, 0.0).astype(F32)
    south_in = jnp.where(lat < n_lat - 1, 1.0, 0.0).astype(F32)
    x = jnp.concatenate(
        [hh_recv[0].astype(F32) * north_in, hh_recv[1].astype(F32) * south_in], axis=1
    )
    root, _, _ = root_of(x)
    edge = (x * root).astype(BF16)
    us[nn : 2 * nn, lanes(0)] = edge[:, :LANES]
    us[nn : 2 * nn, lanes(rpad - 1)] = edge[:, LANES:]

    eu_send[...] = dot(us[nn : 2 * nn, :], sel[...]).astype(BF16)
    eu_copies = [
        go(remote(eu_send, eu_recv.at[0], eu_ss.at[0], eu_rs.at[0], east)),
        go(remote(eu_send, eu_recv.at[1], eu_ss.at[1], eu_rs.at[1], west)),
    ]

    inputs[3].wait()
    order = []
    for p in range(2):
        for a in range(2):
            for v in range(2):
                for q in range(2):
                    b = v if q else 1 - v
                    order.append(4 * (2 * p + q) + 2 * a + b)
    for g in range(4):
        block = jnp.concatenate([w_v[t] for t in order[4 * g : 4 * g + 4]], axis=0)
        wt[:, 4 * chans * g : 4 * chans * (g + 1)] = block.T

    inputs[2].wait()

    def widen(k, c):
        span = chans * rows
        tf[pl.ds(pl.multiple_of(k * span, span), span), :] = (
            tgt_v[k].astype(F32).reshape(span, LANES)
        )
        return c

    lax.fori_loop(0, 4, widen, 0)
    bacc[...] = jnp.zeros_like(bacc)
    gs[0, : 2 * chans, lanes(0)] = jnp.zeros((2 * chans, LANES), BF16)
    gs[1, : 2 * chans, lanes(rpad - 1)] = jnp.zeros((2 * chans, LANES), BF16)

    for c in eu_copies:
        c.wait_recv()
    lane = lax.broadcasted_iota(jnp.int32, (nn, LANES), 1)
    eu_send_mix = jnp.where(lane < 32, eu_recv[0].astype(F32), eu_recv[1].astype(F32))
    eu_mix = eu_send_mix.astype(BF16)

    def shift_u(r, c):
        y = dot(jnp.concatenate([us[nn : 2 * nn, lanes(r)], eu_mix], axis=1), sr[r])
        us[:nn, lanes(r)] = y[:, :LANES].astype(BF16)
        us[2 * nn :, lanes(r)] = y[:, LANES:].astype(BF16)
        return c

    lax.fori_loop(0, rpad, shift_u, 0)

    def recon_tile(it, c):
        t = lax.rem(it + rows // 2 - 1, rows // 2)
        for p in range(2):
            area = [area_ref[lat * 2 * rows + p * rows + 2 * t + i] for i in range(2)]
            for q in range(2):
                phase = 2 * p + q
                moved = jnp.concatenate(
                    [us[q * nn : (q + 2) * nn, lanes(2 * t + p + a, 2)] for a in range(2)], axis=0
                )
                w = jnp.concatenate([w_v[4 * phase + k] for k in range(4)], axis=1)
                recon = dot(w, moved) + bias_col
                total = jnp.zeros((chans, LANES), F32)
                for i in range(2):
                    want = tf[pl.ds(phase * chans * rows + 2 * t + i, chans, stride=rows), :]
                    diff = (recon[:, i * LANES : (i + 1) * LANES] - want) * area[i]
                    total = total + diff
                    gs[p, q * chans : (q + 1) * chans, lanes(2 * t + i + 1)] = diff.astype(BF16)
                bacc[:chans, :] += total
        return c

    lax.fori_loop(0, 2, recon_tile, 0)
    top, bottom = gs.at[0, : 2 * chans], gs.at[1, : 2 * chans]
    grow_copies = [
        go(remote(gs.at[0, 0 : 2 * chans, lanes(1)], gs.at[0, 0 : 2 * chans, lanes(rpad - 1)],
                  grow_ss.at[0], grow_rs.at[0], north)),
        go(remote(gs.at[1, 0 : 2 * chans, lanes(rows)], gs.at[1, 0 : 2 * chans, lanes(0)],
                  grow_ss.at[1], grow_rs.at[1], south)),
    ]
    lax.fori_loop(2, rows // 2, recon_tile, 0)
    for c in grow_copies:
        c.wait_recv()
    gs[0, : 2 * chans, lanes(rpad - 1)] = (
        gs[0, : 2 * chans, lanes(rpad - 1)].astype(F32) * south_in
    ).astype(BF16)
    gs[1, : 2 * chans, lanes(0)] = (
        gs[1, : 2 * chans, lanes(0)].astype(F32) * north_in
    ).astype(BF16)
    for p in range(2):
        eg_send[p] = dot(gs[p, : 2 * chans, :], sel[...]).astype(BF16)
    eg_copies = [
        go(remote(eg_send.at[:, 0:chans], eg_recv.at[:, 0:chans], eg_ss.at[0], eg_rs.at[0], west)),
        go(remote(eg_send.at[:, chans : 2 * chans], eg_recv.at[:, chans : 2 * chans],
                  eg_ss.at[1], eg_rs.at[1], east)),
    ]

    per_tap = chans // half

    def grad_taps(slot, p):
        for q in range(2):
            for a in range(2):
                y = dot_nt(
                    gs[p, q * chans : (q + 1) * chans, lanes(1, rows)],
                    us[q * nn : (q + 2) * nn, lanes(p + a, rows)],
                )
                for b in range(2):
                    for k in range(per_tap):
                        dw[slot, (4 * q + 2 * a + b) * per_tap + k] = y[
                            k * half : (k + 1) * half, b * nn : (b + 1) * nn
                        ]

    grad_taps(0, 1 - core)
    pw = go(remote(dw.at[0], dwp, pw_ss, pw_rs, pair))
    grad_taps(1, core)

    for c in eg_copies:
        c.wait_recv()

    def shift_g(r, c):
        for p in range(2):
            rr = r + 1 - p
            y = dot(jnp.concatenate([gs[p, : 2 * chans, lanes(rr)], eg_recv[p]], axis=1), sr[rr])
            gs[p, 2 * chans : 3 * chans, lanes(rr)] = y[:chans, LANES:].astype(BF16)
            gs[p, 3 * chans :, lanes(rr)] = y[chans:, :LANES].astype(BF16)
        return c

    lax.fori_loop(0, rows + 1, shift_g, 0)

    def grad_rows(k):
        moved = jnp.concatenate(
            [gs[p, :, lanes(2 * k + 2 - p - a, 2)] for p in range(2) for a in range(2)], axis=0
        )
        y = dot(wt[...], moved)
        gu[2 * k] = y[:, :LANES]
        gu[2 * k + 1] = y[:, LANES:]

    far = n_lev // 2
    rs_copies = {}

    def rs_send(way, s, h, first):
        owner = wrap(lev + (far + 1 - s if way else s - far - 1), n_lev)
        row = 2 * owner + h
        if first:
            src = gu.at[row]
        else:
            rs_copies[way, s - 1, h].wait_recv()
            abuf[way, s, h] = gu[row] + arecv[way, s - 1, h]
            src = abuf.at[way, s, h]
        rs_copies[way, s, h] = go(
            remote(src, arecv.at[way, s, h], a_ss.at[way, s, h], a_rs.at[way, s, h],
                   above if way else below)
        )

    grad_rows(wrap(lev + far, n_lev))
    rs_send(0, 1, 0, True)
    rs_send(1, 1, 1, True)
    grad_rows(wrap(lev + far - 1, n_lev))
    rs_send(1, 2, 0, True)
    grad_rows(wrap(lev + far + 1, n_lev))
    rs_send(0, 2, 1, True)

    def over_chips(make):
        def start(j, c):
            make(j).start()
            return c

        def arrive(j, c):
            make(j).wait_recv()
            return c

        def sent(j, c):
            make(j).wait_send()
            return c

        lax.fori_loop(1, n_chip, start, 0)
        return (
            lambda: lax.fori_loop(1, n_chip, arrive, 0),
            lambda: lax.fori_loop(1, n_chip, sent, 0),
        )

    def rb_make(j):
        k = wrap(chip + j, n_chip)
        return remote(rsb.at[k], rsr.at[j], rb_ss.at[j], rb_rs.at[j], at_chip(k))

    pw.wait_recv()

    def join(k, c):
        dw[1, k] = dw[1, k] + dwp[k]
        rsb[k] = dw[1, k].astype(BF16)
        return c

    lax.fori_loop(0, n_chip, join, 0)
    rb_arrive, rb_sent = over_chips(rb_make)

    rs_send(0, 2, 0, False)
    rs_send(1, 2, 1, False)
    grad_rows(wrap(lev + far - 2, n_lev))
    grad_rows(wrap(lev + far + 2, n_lev))
    for way, h in ((0, 1), (1, 0), (0, 0), (1, 1)):
        rs_send(way, 3, h, False)
    grad_rows(wrap(lev + 1, n_lev))
    grad_rows(wrap(lev + n_lev - 1, n_lev))
    grad_rows(lev)

    def mix_tile(t, acc):
        at = lanes(2 * t, 2)
        g = jnp.concatenate([gu[2 * t], gu[2 * t + 1]], axis=1)
        mixing = g * hr_s[:, at]
        m_hi, m_lo = split(mixing)
        mh[:, at] = m_hi
        ml[:, at] = m_lo
        return acc + mixing[:, :LANES] + mixing[:, LANES:]

    msum = lax.fori_loop(0, rows // 2, mix_tile, jnp.zeros((nn, LANES), F32))
    beta_part = jnp.sum(msum, axis=1, keepdims=True)
    bias_part = jnp.sum(bacc[...].T, axis=0, keepdims=True)
    ext[:, :nn] = dot_nt(mh[...], sqh[...]) + (
        dot_nt(ml[...], sqh[...]) + dot_nt(mh[...], sql[...])
    )
    lane = lax.broadcasted_iota(jnp.int32, (nn, LANES), 1)
    ext[:, nn:] = jnp.where(lane == LANES - 1, beta_part, bias_part)
    mine = pl.multiple_of(core * (nn // 2), nn // 2)
    others = pl.multiple_of((1 - core) * (nn // 2), nn // 2)
    pe = go(remote(ext.at[pl.ds(others, nn // 2)], extp, pe_ss, pe_rs, pair))

    for way, h in ((0, 1), (1, 0), (0, 0), (1, 1)):
        rs_send(way, 4, h, False)

    rb_arrive()

    def add_taps(j, acc):
        return acc + rsr[j].astype(F32)

    wg[core, chip] = lax.fori_loop(1, n_chip, add_taps, dw[1, chip]) * (1.0 / total_cells)

    def ab_make(j):
        k = wrap(chip + j, n_chip)
        return remote(
            wg.at[core, chip], wg.at[core, chip], ab_ss.at[j], ab_rs.at[j], at_chip(k)
        )

    ab_arrive, ab_sent = over_chips(ab_make)

    pe.wait_recv()

    def join_ext(k, c):
        at = pl.ds(pl.multiple_of(mine + k * share, share), share)
        exts[k] = ext[at, :] + extp[pl.ds(pl.multiple_of(k * share, share), share), :]
        return c

    lax.fori_loop(0, n_chip, join_ext, 0)
    extr[chip] = exts[chip]

    def rc_make(j):
        k = wrap(chip + j, n_chip)
        return remote(exts.at[k], extr.at[chip], rc_ss.at[j], rc_rs.at[j], at_chip(k))

    rc_arrive, rc_sent = over_chips(rc_make)

    for way in range(2):
        for h in range(2):
            rs_copies[way, 4, h].wait_recv()
    g = jnp.concatenate(
        [gu[2 * lev + h] + (arecv[0, 4, h] + arecv[1, 4, h]) for h in range(2)], axis=1
    )
    at = lanes(2 * lev, 2)
    m_hi, m_lo = split(g * hr_s[:, at])
    back = dot(gt3[...], jnp.concatenate([m_hi, m_hi, m_lo], axis=0))
    gh = (g * root_s[:, at] + 2.0 * hx[:, lanes(2 * lev + 1, 2)] * back).astype(BF16)
    agr[2 * lev] = gh[:, :LANES]
    agr[2 * lev + 1] = gh[:, LANES:]

    ag_copies = {}

    def ag_send(s):
        for way in range(2):
            for h in range(2):
                if s == far and h != way:
                    continue
                if s > 1:
                    ag_copies[way, s - 1, h].wait_recv()
                owner = wrap(lev + (1 - s if way else s - 1), n_lev)
                block = agr.at[2 * owner + h]
                ag_copies[way, s, h] = go(
                    remote(block, block, g_ss.at[way, s, h], g_rs.at[way, s, h],
                           above if way else below)
                )

    def put(owner, h):
        row = 2 * owner + h
        gho[pl.ds(row, nn, stride=rows), :] = agr[row].astype(F32)

    def put_step(s):
        for way in range(2):
            for h in range(2):
                put(wrap(lev + (-s if way else s), n_lev), h)

    ag_send(1)
    put(lev, 0)
    put(lev, 1)

    rc_arrive()

    def add_ext(k, acc):
        return acc + extr[k]

    plane = lax.fori_loop(1, n_chip, add_ext, extr[0])
    gb_out[...] = plane[0:1, nn : nn + chans] * (1.0 / total_cells)
    extz[lev] = plane

    def z_make(j):
        return remote(
            extz.at[lev], extz.at[lev], z_ss.at[j], z_rs.at[j], (lat, lon, wrap(lev + j, n_lev))
        )

    for j in range(1, n_lev):
        z_make(j).start()

    ag_send(2)
    put_step(1)

    ab_arrive()
    pg = go(remote(wg.at[core], wg.at[core], pg_ss, pg_rs, pair))
    for j in range(1, n_lev):
        z_make(j).wait_recv()
    whole = extz[0]
    for k in range(1, n_lev):
        whole = whole + extz[k]
    extg[core, chip] = whole * (1.0 / total_cells)

    def ac_make(j):
        k = wrap(chip + j, n_chip)
        return remote(
            extg.at[core, chip], extg.at[core, chip], ac_ss.at[j], ac_rs.at[j], at_chip(k)
        )

    ac_arrive, ac_sent = over_chips(ac_make)
    ag_send(3)
    put_step(2)
    ac_arrive()
    pc = go(remote(extg.at[core], extg.at[core], pc_ss, pc_rs, pair))
    ag_send(4)
    for way in range(2):
        ag_copies[way, 3, 1 - way].wait_recv()
    put_step(3)
    pg.wait_recv()
    gw_copy = pltpu.make_async_copy(wg, gw_out, out_sem.at[0])
    gw_copy.start()
    pc.wait_recv()
    full = extg[...].reshape(nn, nn + LANES)
    gg_out[...] = full[:, :nn]
    gbeta_out[...] = jnp.sum(
        jnp.where(eye, full[:, nn + LANES - 1 : nn + LANES], 0.0), axis=0, keepdims=True
    )
    for way in range(2):
        ag_copies[way, far, way].wait_recv()
        put(wrap(lev + far, n_lev), way)
    gh_copy = pltpu.make_async_copy(gho, gh_out, out_sem.at[1])
    gh_copy.start()

    for c in sends:
        c.wait_send()
    rb_sent()
    ab_sent()
    rc_sent()
    ac_sent()
    for j in range(1, n_lev):
        z_make(j).wait_send()
    gw_copy.wait()
    gh_copy.wait()


def local(sizes, target, hidden, weight, bias, gamma, beta):
    n_lat, n_lon, n_lev = sizes
    nn, rows, cols = hidden.shape
    chans = weight.shape[1]
    taps = weight.shape[0]
    n_chip = n_lat // 2 * n_lon
    half = taps // 2 * chans // n_chip
    share = nn // 2 // n_chip
    cells = rows * cols
    rpad = rows + 2
    total_rows = rows * n_lat
    total_cells = total_rows * cols * n_lon
    far = n_lev // 2
    at = np.arange(total_rows).reshape(n_lat, 1, rows) * 2.0 + np.arange(2).reshape(1, 2, 1)
    area = np.cos(math.pi * ((at + 0.5) / (2.0 * total_rows) - 0.5)).astype(np.float32)
    dims = (nn, rows, chans, n_lat, n_lon, n_lev, 4, total_cells)
    wide = nn + LANES
    V = pltpu.VMEM
    D = pltpu.SemaphoreType.DMA
    scratch = [
        V((nn, rows, cols), BF16), V((4, chans, rows, cols), BF16), V((taps, chans, nn), BF16),
        V((nn, nn), F32),
        V((nn * rows, cols), F32), V((4 * chans * rows, cols), F32), V((nn, rpad * cols), F32),
        V((nn, cells), F32), V((nn, cells), F32), V((nn, cells), BF16), V((nn, cells), BF16),
        V((nn, 3 * nn), BF16), V((nn, 3 * nn), BF16), V((nn, taps * chans), BF16),
        V((3 * nn, rpad * cols), BF16), V((2, 4 * chans, rpad * cols), BF16),
        V((rpad * cols, cols), BF16), V((rpad, 2 * cols, 2 * cols), BF16),
        V((2, nn, cols), BF16), V((2, nn, cols), BF16), V((nn, cols), BF16),
        V((2, nn, cols), BF16), V((2, 2 * chans, cols), BF16), V((2, 2 * chans, cols), BF16),
        V((2, n_chip, half, nn), F32), V((n_chip, half, nn), F32), V((n_chip, half, nn), BF16),
        V((n_chip, half, nn), BF16), V((2, n_chip, half, nn), F32),
        V((rows, nn, cols), F32), V((cols, cols), F32), V((nn, cells), BF16), V((nn, cells), BF16),
        V((nn, wide), F32), V((nn // 2, wide), F32), V((n_chip, share, wide), F32),
        V((n_chip, share, wide), F32), V((n_lev, share, wide), F32),
        V((2, n_chip, share, wide), F32),
        V((2, far + 1, 2, nn, cols), F32), V((2, far + 1, 2, nn, cols), F32),
        V((rows, nn, cols), BF16), V((nn * rows, cols), F32),
        D((4,)), D((2,)),
        D((2,)), D((2,)), D((2,)), D((2,)), D((2,)), D((2,)), D((2,)), D((2,)),
        D, D, D((n_chip,)), D((n_chip,)), D((n_chip,)), D((n_chip,)), D, D,
        D, D, D((n_chip,)), D((n_chip,)), D((n_lev,)), D((n_lev,)), D((n_chip,)), D((n_chip,)),
        D, D,
        D((2, far + 1, 2)), D((2, far + 1, 2)), D((2, far + 1, 2)), D((2, far + 1, 2)),
    ]
    hbm = pl.BlockSpec(memory_space=pl.ANY)
    vmem = pl.BlockSpec(memory_space=pltpu.VMEM)
    smem = pl.BlockSpec(memory_space=pltpu.SMEM)
    gh, gw, gb, gg, gbeta = pl.pallas_call(
        functools.partial(kernel, dims),
        out_shape=(
            jax.ShapeDtypeStruct((nn * rows, cols), F32),
            jax.ShapeDtypeStruct((2, n_chip, half, nn), F32),
            jax.ShapeDtypeStruct((1, chans), F32),
            jax.ShapeDtypeStruct((nn, nn), F32),
            jax.ShapeDtypeStruct((1, nn), F32),
        ),
        in_specs=[smem, hbm, hbm, hbm, vmem, hbm, vmem],
        out_specs=(hbm, hbm, vmem, vmem, vmem),
        scratch_shapes=scratch,
        compiler_params=pltpu.CompilerParams(
            collective_id=0, has_side_effects=True, vmem_limit_bytes=60 * 2**20
        ),
    )(
        jnp.asarray(area.reshape(-1)), hidden, target, weight, bias.reshape(1, chans),
        gamma, beta.reshape(1, nn),
    )
    return (
        gh.reshape(nn, rows, cols), gw.reshape(taps, chans, nn), gb.reshape(chans), gg,
        gbeta.reshape(nn),
    )


def solution(mesh):
    sizes = tuple(mesh.shape[a] for a in ("lat", "lon", "lev"))
    return jax.shard_map(
        functools.partial(local, sizes),
        mesh=mesh,
        in_specs=(
            P(None, "lev", "lat", "lon"),
            P(None, "lat", "lon"),
            P(None, "lev", None),
            P("lev"),
            P(),
            P(),
        ),
        out_specs=(P(None, "lat", "lon"), P(None, "lev", None), P("lev"), P(), P()),
        check_vma=False,
    )
```

time: 391 us -> 97.4 us (0.25); the launches traced: 384 us -> 95.5 us
  waiting for transfers between devices: 126 us -> 0 us
  Pallas kernels: 0 us -> 88.8 us
  local copies, waits for them, and re-layouts: 89 us -> 6.1 us
  blocking collectives: 63.1 us -> 0 us
  starting transfers between devices: 33.1 us -> 0 us
  matrix products: 30.7 us -> 0 us
  other arithmetic: 27.3 us -> 0 us
  between operations: 15 us -> 0.66 us
    psum x2 -> x0, waiting for transfers between devices: 120 us -> none  [the longest x1 77.2 us: local(): grad_u = lax.psum(grad_part, 'lev')]
    pallas_call x0 -> x1, Pallas kernels: none -> 88.8 us  [local(): pl.pallas_call(functools.partial(kernel, dims), out_shape=(jax.ShapeDtype...]
    psum x1 -> x0, blocking collectives: 63.1 us -> none  [local(): lax.psum((jnp.concatenate(weight_parts, axis=0), bias_sum), ('lat', 'lon'))]
    slice x23 -> x0, local copies, waits for them, and re-layouts: 56.1 us -> none  [the longest x22 56 us: window(): return field[:, 1 + drow:1 + drow + rows, 1 + dcol:1 + dcol + cols]]
    ppermute x8 -> x0, starting transfers between devices: 33 us -> none  [the longest x4 27.5 us: extended(): after = lax.ppermute(initial, axis, down)]
    dot_general x12 -> x0, matrix products: 30.7 us -> none  [the longest x4 6.34 us: local(): lax.dot_general(kernel, moved, (((0, 2), (0, 1)), ((), ())), preferred_el...]
    unnamed x118 -> x13, local copies, waits for them, and re-layouts: 19.5 us -> 6.1 us
    another operation x4 -> x0, local copies, waits for them, and re-layouts: 9.6 us -> none  [local(): residual = jnp.stack(residuals, axis=0)]
  transfers between devices with their start and end apart: 10 -> 0, of which waited for: 5 -> 0; matrix products, arithmetic and copies ran while one was open for 5% -> 0% of each run, Pallas kernels for 0% -> 0%
where the time goes in v1:
time: 97.4 us; the launch traced here: 95.5 us
  Pallas kernels  88.8 us (91%)
  local copies, waits for them, and re-layouts  6.1 us (6%)
    pallas_call x1, Pallas kernels, local(): pl.pallas_call(functools.partial(kernel, dims), out_shape=(jax.ShapeDtype...  88.8 us
    unnamed x13, local copies, waits for them, and re-layouts  6.1 us

profile of v1, /device:TPU:6, one launch (start us, length us, event | category | flops | bytes accessed | tf_op | source)
XLA Modules:
  0.0 95.5 jit_solution(9771292363304496)
XLA Ops:
  0.6 88.8 %shard_map.110 = (f32[4096,128]{1,0:T(8,128)}, f32[2,16,48,256]{3,2,1,0:T(8,128)}, f32[1,96]{1,0:T(1,128)}, f32[256,256]{1,0:T(8,128)}, f32[1,256]{1,0:T(1,128)}) custom-call(f32[128]{0:T(128)} %constant.2.clone.area_ref, bf16[256,16,128]{2,1,0:T(8,128)(2,1)} %hidden_ref.1, bf16[4,96,16,128]{3,2,1,0:T(8,128)(2,1)} %target_ref.1, ...), custom_call_target="tpu_custom_call" | custom-call | tf_op jit(solution)/shard_map/pallas_call | solution.py:616
  89.4 0.0 copy-start
  89.4 3.2 %copy.17 = f32[256,16,128]{2,1,0:T(8,128)} copy(f32[256,16,128]{2,1,0:T(8,128)} %bitcast.6) | data formatting | bytes 4194304
  92.6 0.0 copy-done
  92.6 0.0 copy-start.3
  92.6 0.0 copy-start.1
  92.6 0.0 copy-start.2
  92.6 1.1 %copy.18 = f32[16,96,256]{2,1,0:T(8,128)} copy(f32[16,96,256]{2,1,0:T(8,128)S(1)} %bitcast.7) | data formatting | bytes 3145728
  93.7 0.0 copy-done.3
  93.8 0.5 copy.19
  94.3 0.0 copy-done.1
  94.3 0.7 copy.20
  95.0 0.0 copy-done.2
  95.0 0.6 copy.21
Async XLA Ops:
  89.4 3.2 %copy-start = (f32[2,16,48,256]{3,2,1,0:T(8,128)S(1)}, f32[2,16,48,256]{3,2,1,0:T(8,128)}, u32[]{:S(2)}) copy-start(f32[2,16,48,256]{3,2,1,0:T(8,128)} %get-tuple-element.11) | copy-start | bytes 4718596
  92.6 1.2 %copy-start.3 = (f32[1,96]{1,0:T(1,128)S(1)}, f32[1,96]{1,0:T(1,128)}, u32[]{:S(2)}) copy-start(f32[1,96]{1,0:T(1,128)} %get-tuple-element.12) | copy-start | bytes 1156
  92.6 1.7 %copy-start.1 = (f32[256,256]{1,0:T(8,128)S(1)}, f32[256,256]{1,0:T(8,128)}, u32[]{:S(2)}) copy-start(f32[256,256]{1,0:T(8,128)} %get-tuple-element.23) | copy-start | bytes 786436
  92.6 2.4 %copy-start.2 = (f32[1,256]{1,0:T(1,128)S(1)}, f32[1,256]{1,0:T(1,128)}, u32[]{:S(2)}) copy-start(f32[1,256]{1,0:T(1,128)} %get-tuple-element.14) | copy-start | bytes 3076

commit v2 on v1

--- a/solution.py
+++ b/solution.py
@@ -35,14 +35,13 @@
 def kernel(
     dims,
     area_ref, hidden_ref, target_ref, weight_ref, bias_ref, gamma_ref, beta_ref,
-    gh_out, gw_out, gb_out, gg_out, gbeta_out,
+    gh_out, gw_out, ext_out, gb_out,
     hid_v, tgt_v, w_v, gamma_v,
     hf, tf, hx, root_s, hr_s, sqh, sql, g3, gt3, wt,
-    us, gs, sel, sr,
-    hh_send, hh_recv, eu_send, eu_recv, eg_send, eg_recv,
-    dw, dwp, rsb, rsr, wg,
-    gu, bacc, mh, ml, ext, extp, exts, extr, extz, extg,
-    abuf, arecv, agr, gho,
+    us, gs, sel, eu_send, eu_recv, eg_send, eg_recv, eg_corner,
+    dw, dwp, rsb, rsr, wown,
+    gu, bacc, mh, ml, ext, extp, exts, extr, extz, eown,
+    abuf, arecv, ghown,
     in_sem, out_sem,
     row_ss, row_rs, eu_ss, eu_rs, grow_ss, grow_rs, eg_ss, eg_rs,
     pw_ss, pw_rs, rb_ss, rb_rs, ab_ss, ab_rs, pg_ss, pg_rs,
@@ -96,8 +95,12 @@
     def greet(device):
         pl.semaphore_signal(barrier, inc=1, device_id=device, device_id_type=MESH)
 
-    greet(pair)
-    greet((n_lat - 1 - lat, lon, lev))
+    corners = [
+        (wrap(lat + i, n_lat), wrap(lon + j, n_lon), lev) for i in (-1, 1) for j in (-1, 1)
+    ]
+    northwest, northeast, southwest, southeast = corners
+    for device in [north, south] + corners:
+        greet(device)
 
     def greet_chip(j, c):
         greet(at_chip(wrap(chip + j, n_chip)))
@@ -119,40 +122,17 @@
         return c
 
     lax.fori_loop(0, rows, spread, 0)
-    hh_send[0] = hx[:, lanes(1)].astype(BF16)
-    hh_send[1] = hx[:, lanes(rows)].astype(BF16)
-    pl.semaphore_wait(barrier, 2 + (n_chip - 1) + (n_lev - 1))
-
-    sends = []
-
-    def go(copy):
-        copy.start()
-        sends.append(copy)
-        return copy
-
-    row_copies = [
-        go(remote(hh_send.at[0], hh_recv.at[1], row_ss.at[0], row_rs.at[0], north)),
-        go(remote(hh_send.at[1], hh_recv.at[0], row_ss.at[1], row_rs.at[1], south)),
-    ]
-
     def make_sel(r, c):
         k = lax.broadcasted_iota(jnp.int32, (LANES, LANES), 0)
         e = lax.broadcasted_iota(jnp.int32, (LANES, LANES), 1)
-        hit = ((k == LANES - 1) & (e == r)) | ((k == 0) & (e == 32 + r))
-        sel[lanes(r), :] = jnp.where(hit, 1.0, 0.0).astype(BF16)
-        ki = lax.broadcasted_iota(jnp.int32, (2 * LANES, 2 * LANES), 0)
-        o = lax.broadcasted_iota(jnp.int32, (2 * LANES, 2 * LANES), 1)
-        low = ki < LANES
-        hit = (
-            (low & (o < LANES) & (ki == o - 1))
-            | (low & (o >= LANES) & (ki == o - LANES + 1))
-            | ((o == 0) & (ki == LANES + r))
-            | ((o == 2 * LANES - 1) & (ki == LANES + 32 + r))
-        )
-        sr[r] = jnp.where(hit, 1.0, 0.0).astype(BF16)
-        return c
-
-    lax.fori_loop(0, rpad, make_sel, 0)
+        last, first = k == LANES - 1, k == 0
+        hit = (last & (e == r)) | (first & (e == 32 + r))
+        hit = hit | ((r == rows) & ((last & (e == 0)) | (first & (e == 32))))
+        hit = hit | ((r == 1) & ((last & (e == rows + 1)) | (first & (e == 33 + rows))))
+        sel[lanes(r - 1), :] = jnp.where(hit, 1.0, 0.0).astype(BF16)
+        return c
+
+    lax.fori_loop(1, rows + 1, make_sel, 0)
 
     inputs[1].wait()
     gamma = gamma_v[...]
@@ -185,24 +165,30 @@
         us[nn : 2 * nn, lanes(2 * t + 1, 2)] = (x * root).astype(BF16)
         return c
 
-    lax.fori_loop(0, rows // 2, root_tile, 0)
-
-    for c in row_copies:
-        c.wait_recv()
+    lax.fori_loop(0, rows // 2, root_tile, 0, unroll=2)
+
     north_in = jnp.where(lat > 0, 1.0, 0.0).astype(F32)
     south_in = jnp.where(lat < n_lat - 1, 1.0, 0.0).astype(F32)
-    x = jnp.concatenate(
-        [hh_recv[0].astype(F32) * north_in, hh_recv[1].astype(F32) * south_in], axis=1
-    )
-    root, _, _ = root_of(x)
-    edge = (x * root).astype(BF16)
-    us[nn : 2 * nn, lanes(0)] = edge[:, :LANES]
-    us[nn : 2 * nn, lanes(rpad - 1)] = edge[:, LANES:]
-
-    eu_send[...] = dot(us[nn : 2 * nn, :], sel[...]).astype(BF16)
+    eu_send[...] = dot(us[nn : 2 * nn, lanes(1, rows)], sel[...]).astype(BF16)
+
+    pl.semaphore_wait(barrier, 6 + (n_chip - 1) + (n_lev - 1))
+
+    sends = []
+
+    def go(copy):
+        copy.start()
+        sends.append(copy)
+        return copy
+
+    mid = slice(nn, 2 * nn)
     eu_copies = [
-        go(remote(eu_send, eu_recv.at[0], eu_ss.at[0], eu_rs.at[0], east)),
-        go(remote(eu_send, eu_recv.at[1], eu_ss.at[1], eu_rs.at[1], west)),
+        go(remote(us.at[mid, lanes(1)], us.at[mid, lanes(rpad - 1)],
+                  row_ss.at[0], row_rs.at[0], north)),
+        go(remote(us.at[mid, lanes(rows)], us.at[mid, lanes(0)],
+                  row_ss.at[1], row_rs.at[1], south)),
+    ] + [
+        go(remote(eu_send, eu_recv.at[i], eu_ss.at[i], eu_rs.at[i], device))
+        for i, device in enumerate((east, west, southeast, southwest, northeast, northwest))
     ]
 
     inputs[3].wait()
@@ -233,17 +219,31 @@
 
     for c in eu_copies:
         c.wait_recv()
+    us[mid, lanes(0)] = (us[mid, lanes(0)].astype(F32) * north_in).astype(BF16)
+    us[mid, lanes(rpad - 1)] = (us[mid, lanes(rpad - 1)].astype(F32) * south_in).astype(BF16)
     lane = lax.broadcasted_iota(jnp.int32, (nn, LANES), 1)
-    eu_send_mix = jnp.where(lane < 32, eu_recv[0].astype(F32), eu_recv[1].astype(F32))
-    eu_mix = eu_send_mix.astype(BF16)
+    eu_mix = jnp.where(lane < 32, eu_recv[0].astype(F32), eu_recv[1].astype(F32))
+    for i, at, keep in (
+        (2, 0, north_in), (3, 32, north_in), (4, rows + 1, south_in), (5, rows + 33, south_in)
+    ):
+        eu_mix = jnp.where(lane == at, eu_recv[i].astype(F32) * keep, eu_mix)
+
+    def from_west(x, e, r):
+        at = lax.broadcasted_iota(jnp.int32, x.shape, 1)
+        return jnp.where(at == 0, pltpu.roll(e, LANES - r, 1), pltpu.roll(x, 1, 1))
+
+    def from_east(x, e, r):
+        at = lax.broadcasted_iota(jnp.int32, x.shape, 1)
+        edge = pltpu.roll(e, LANES - 33 - r, 1)
+        return jnp.where(at == LANES - 1, edge, pltpu.roll(x, LANES - 1, 1))
 
     def shift_u(r, c):
-        y = dot(jnp.concatenate([us[nn : 2 * nn, lanes(r)], eu_mix], axis=1), sr[r])
-        us[:nn, lanes(r)] = y[:, :LANES].astype(BF16)
-        us[2 * nn :, lanes(r)] = y[:, LANES:].astype(BF16)
-        return c
-
-    lax.fori_loop(0, rpad, shift_u, 0)
+        x = us[mid, lanes(r)].astype(F32)
+        us[:nn, lanes(r)] = from_west(x, eu_mix, r).astype(BF16)
+        us[2 * nn :, lanes(r)] = from_east(x, eu_mix, r).astype(BF16)
+        return c
+
+    lax.fori_loop(0, rpad, shift_u, 0, unroll=3)
 
     def recon_tile(it, c):
         t = lax.rem(it + rows // 2 - 1, rows // 2)
@@ -265,29 +265,27 @@
                 bacc[:chans, :] += total
         return c
 
-    lax.fori_loop(0, 2, recon_tile, 0)
-    top, bottom = gs.at[0, : 2 * chans], gs.at[1, : 2 * chans]
+    lax.fori_loop(0, 2, recon_tile, 0, unroll=2)
     grow_copies = [
         go(remote(gs.at[0, 0 : 2 * chans, lanes(1)], gs.at[0, 0 : 2 * chans, lanes(rpad - 1)],
                   grow_ss.at[0], grow_rs.at[0], north)),
         go(remote(gs.at[1, 0 : 2 * chans, lanes(rows)], gs.at[1, 0 : 2 * chans, lanes(0)],
                   grow_ss.at[1], grow_rs.at[1], south)),
     ]
-    lax.fori_loop(2, rows // 2, recon_tile, 0)
-    for c in grow_copies:
-        c.wait_recv()
-    gs[0, : 2 * chans, lanes(rpad - 1)] = (
-        gs[0, : 2 * chans, lanes(rpad - 1)].astype(F32) * south_in
-    ).astype(BF16)
-    gs[1, : 2 * chans, lanes(0)] = (
-        gs[1, : 2 * chans, lanes(0)].astype(F32) * north_in
-    ).astype(BF16)
+    lax.fori_loop(2, rows // 2, recon_tile, 0, unroll=2)
     for p in range(2):
-        eg_send[p] = dot(gs[p, : 2 * chans, :], sel[...]).astype(BF16)
+        eg_send[p] = dot(gs[p, : 2 * chans, lanes(1, rows)], sel[...]).astype(BF16)
+    east_part, west_part = slice(0, chans), slice(chans, 2 * chans)
     eg_copies = [
-        go(remote(eg_send.at[:, 0:chans], eg_recv.at[:, 0:chans], eg_ss.at[0], eg_rs.at[0], west)),
-        go(remote(eg_send.at[:, chans : 2 * chans], eg_recv.at[:, chans : 2 * chans],
-                  eg_ss.at[1], eg_rs.at[1], east)),
+        go(remote(src, dst, eg_ss.at[i], eg_rs.at[i], device))
+        for i, (src, dst, device) in enumerate((
+            (eg_send.at[:, east_part], eg_recv.at[:, east_part], west),
+            (eg_send.at[:, west_part], eg_recv.at[:, west_part], east),
+            (eg_send.at[0, east_part], eg_corner.at[0, east_part], northwest),
+            (eg_send.at[0, west_part], eg_corner.at[0, west_part], northeast),
+            (eg_send.at[1, east_part], eg_corner.at[1, east_part], southwest),
+            (eg_send.at[1, west_part], eg_corner.at[1, west_part], southeast),
+        ))
     ]
 
     per_tap = chans // half
@@ -307,28 +305,50 @@
 
     grad_taps(0, 1 - core)
     pw = go(remote(dw.at[0], dwp, pw_ss, pw_rs, pair))
-    grad_taps(1, core)
-
-    for c in eg_copies:
+
+    for c in grow_copies + eg_copies:
         c.wait_recv()
+    gs[0, : 2 * chans, lanes(rpad - 1)] = (
+        gs[0, : 2 * chans, lanes(rpad - 1)].astype(F32) * south_in
+    ).astype(BF16)
+    gs[1, : 2 * chans, lanes(0)] = (
+        gs[1, : 2 * chans, lanes(0)].astype(F32) * north_in
+    ).astype(BF16)
+    lane = lax.broadcasted_iota(jnp.int32, (2 * chans, LANES), 1)
+    eg_mix = []
+    for p, at, keep in ((0, rows + 1, south_in), (1, 0, north_in)):
+        corner = eg_corner[p].astype(F32) * keep
+        eg_mix.append(
+            jnp.where((lane == at) | (lane == at + 32), corner, eg_recv[p].astype(F32))
+        )
 
     def shift_g(r, c):
         for p in range(2):
             rr = r + 1 - p
-            y = dot(jnp.concatenate([gs[p, : 2 * chans, lanes(rr)], eg_recv[p]], axis=1), sr[rr])
-            gs[p, 2 * chans : 3 * chans, lanes(rr)] = y[:chans, LANES:].astype(BF16)
-            gs[p, 3 * chans :, lanes(rr)] = y[chans:, :LANES].astype(BF16)
+            x = gs[p, : 2 * chans, lanes(rr)].astype(F32)
+            gs[p, 2 * chans : 3 * chans, lanes(rr)] = from_east(
+                x[:chans], eg_mix[p][:chans], rr
+            ).astype(BF16)
+            gs[p, 3 * chans :, lanes(rr)] = from_west(
+                x[chans:], eg_mix[p][chans:], rr
+            ).astype(BF16)
         return c
 
     lax.fori_loop(0, rows + 1, shift_g, 0)
 
-    def grad_rows(k):
+    def grad_rows(*chunks):
         moved = jnp.concatenate(
-            [gs[p, :, lanes(2 * k + 2 - p - a, 2)] for p in range(2) for a in range(2)], axis=0
+            [
+                jnp.concatenate([gs[p, :, lanes(2 * k + 2 - p - a, 2)] for k in chunks], axis=1)
+                for p in range(2)
+                for a in range(2)
+            ],
+            axis=0,
         )
         y = dot(wt[...], moved)
-        gu[2 * k] = y[:, :LANES]
-        gu[2 * k + 1] = y[:, LANES:]
+        for i, k in enumerate(chunks):
+            gu[2 * k] = y[:, 2 * i * LANES : (2 * i + 1) * LANES]
+            gu[2 * k + 1] = y[:, (2 * i + 1) * LANES : (2 * i + 2) * LANES]
 
     far = n_lev // 2
     rs_copies = {}
@@ -350,10 +370,10 @@
     grad_rows(wrap(lev + far, n_lev))
     rs_send(0, 1, 0, True)
     rs_send(1, 1, 1, True)
-    grad_rows(wrap(lev + far - 1, n_lev))
+    grad_rows(wrap(lev + far - 1, n_lev), wrap(lev + far + 1, n_lev))
     rs_send(1, 2, 0, True)
-    grad_rows(wrap(lev + far + 1, n_lev))
     rs_send(0, 2, 1, True)
+    grad_taps(1, core)
 
     def over_chips(make):
         def start(j, c):
@@ -378,6 +398,9 @@
         k = wrap(chip + j, n_chip)
         return remote(rsb.at[k], rsr.at[j], rb_ss.at[j], rb_rs.at[j], at_chip(k))
 
+    rs_send(0, 2, 0, False)
+    rs_send(1, 2, 1, False)
+    grad_rows(wrap(lev + far - 2, n_lev), wrap(lev + far + 2, n_lev))
     pw.wait_recv()
 
     def join(k, c):
@@ -388,14 +411,9 @@
     lax.fori_loop(0, n_chip, join, 0)
     rb_arrive, rb_sent = over_chips(rb_make)
 
-    rs_send(0, 2, 0, False)
-    rs_send(1, 2, 1, False)
-    grad_rows(wrap(lev + far - 2, n_lev))
-    grad_rows(wrap(lev + far + 2, n_lev))
     for way, h in ((0, 1), (1, 0), (0, 0), (1, 1)):
         rs_send(way, 3, h, False)
-    grad_rows(wrap(lev + 1, n_lev))
-    grad_rows(wrap(lev + n_lev - 1, n_lev))
+    grad_rows(wrap(lev + 1, n_lev), wrap(lev + n_lev - 1, n_lev))
     grad_rows(lev)
 
     def mix_tile(t, acc):
@@ -427,12 +445,14 @@
     def add_taps(j, acc):
         return acc + rsr[j].astype(F32)
 
-    wg[core, chip] = lax.fori_loop(1, n_chip, add_taps, dw[1, chip]) * (1.0 / total_cells)
+    wown[...] = lax.fori_loop(1, n_chip, add_taps, dw[1, chip]) * (1.0 / total_cells)
+    own_copies = [pltpu.make_async_copy(wown, gw_out.at[core, chip], out_sem.at[0])]
+    own_copies[0].start()
 
     def ab_make(j):
         k = wrap(chip + j, n_chip)
         return remote(
-            wg.at[core, chip], wg.at[core, chip], ab_ss.at[j], ab_rs.at[j], at_chip(k)
+            wown, gw_out.at[core, chip], ab_ss.at[j], ab_rs.at[j], at_chip(k)
         )
 
     ab_arrive, ab_sent = over_chips(ab_make)
@@ -463,37 +483,32 @@
     m_hi, m_lo = split(g * hr_s[:, at])
     back = dot(gt3[...], jnp.concatenate([m_hi, m_hi, m_lo], axis=0))
     gh = (g * root_s[:, at] + 2.0 * hx[:, lanes(2 * lev + 1, 2)] * back).astype(BF16)
-    agr[2 * lev] = gh[:, :LANES]
-    agr[2 * lev + 1] = gh[:, LANES:]
+    ghown[0] = gh[:, :LANES]
+    ghown[1] = gh[:, LANES:]
+    own_copies.append(
+        pltpu.make_async_copy(ghown, gh_out.at[pl.ds(2 * lev, 2)], out_sem.at[1])
+    )
+    own_copies[1].start()
 
     ag_copies = {}
 
-    def ag_send(s):
-        for way in range(2):
-            for h in range(2):
-                if s == far and h != way:
-                    continue
-                if s > 1:
-                    ag_copies[way, s - 1, h].wait_recv()
-                owner = wrap(lev + (1 - s if way else s - 1), n_lev)
-                block = agr.at[2 * owner + h]
-                ag_copies[way, s, h] = go(
-                    remote(block, block, g_ss.at[way, s, h], g_rs.at[way, s, h],
-                           above if way else below)
-                )
-
-    def put(owner, h):
-        row = 2 * owner + h
-        gho[pl.ds(row, nn, stride=rows), :] = agr[row].astype(F32)
-
-    def put_step(s):
-        for way in range(2):
-            for h in range(2):
-                put(wrap(lev + (-s if way else s), n_lev), h)
-
-    ag_send(1)
-    put(lev, 0)
-    put(lev, 1)
+    def ag_send(way, hops, origin, kind, src=None):
+        step = hops if way else -hops
+        owner = wrap(lev - origin if way else lev + origin, n_lev)
+        if kind == 2:
+            rows_of = pl.ds(2 * owner, 2)
+        else:
+            rows_of = pl.ds(2 * owner + kind, 1)
+        block = gh_out.at[rows_of]
+        ag_copies[way, hops + origin] = go(
+            remote(block if src is None else src, block, g_ss.at[way, hops + origin],
+                   g_rs.at[way, hops + origin], (lat, lon, wrap(lev + step, n_lev)))
+        )
+
+    for way in range(2):
+        ag_send(way, 1, 0, 2, ghown)
+    for way in range(2):
+        ag_send(way, 2, 0, 2, ghown)
 
     rc_arrive()
 
@@ -512,47 +527,41 @@
     for j in range(1, n_lev):
         z_make(j).start()
 
-    ag_send(2)
-    put_step(1)
+    for way in range(2):
+        ag_copies[way, 1].wait_recv()
+        ag_send(way, 2, 1, 2)
 
     ab_arrive()
-    pg = go(remote(wg.at[core], wg.at[core], pg_ss, pg_rs, pair))
+    own_copies[0].wait()
+    pg = go(remote(gw_out.at[core], gw_out.at[core], pg_ss, pg_rs, pair))
+
+    for way in range(2):
+        ag_copies[way, 2].wait_recv()
+        ag_send(way, 2, 2, way)
+
     for j in range(1, n_lev):
         z_make(j).wait_recv()
     whole = extz[0]
     for k in range(1, n_lev):
         whole = whole + extz[k]
-    extg[core, chip] = whole * (1.0 / total_cells)
+    eown[...] = whole * (1.0 / total_cells)
+    own_copies.append(pltpu.make_async_copy(eown, ext_out.at[core, chip], out_sem.at[2]))
+    own_copies[2].start()
 
     def ac_make(j):
         k = wrap(chip + j, n_chip)
-        return remote(
-            extg.at[core, chip], extg.at[core, chip], ac_ss.at[j], ac_rs.at[j], at_chip(k)
-        )
+        return remote(eown, ext_out.at[core, chip], ac_ss.at[j], ac_rs.at[j], at_chip(k))
 
     ac_arrive, ac_sent = over_chips(ac_make)
-    ag_send(3)
-    put_step(2)
     ac_arrive()
-    pc = go(remote(extg.at[core], extg.at[core], pc_ss, pc_rs, pair))
-    ag_send(4)
+    own_copies[2].wait()
+    pc = go(remote(ext_out.at[core], ext_out.at[core], pc_ss, pc_rs, pair))
+    pg.wait_recv()
     for way in range(2):
-        ag_copies[way, 3, 1 - way].wait_recv()
-    put_step(3)
-    pg.wait_recv()
-    gw_copy = pltpu.make_async_copy(wg, gw_out, out_sem.at[0])
-    gw_copy.start()
+        ag_copies[way, 3].wait_recv()
+        ag_copies[way, 4].wait_recv()
     pc.wait_recv()
-    full = extg[...].reshape(nn, nn + LANES)
-    gg_out[...] = full[:, :nn]
-    gbeta_out[...] = jnp.sum(
-        jnp.where(eye, full[:, nn + LANES - 1 : nn + LANES], 0.0), axis=0, keepdims=True
-    )
-    for way in range(2):
-        ag_copies[way, far, way].wait_recv()
-        put(wrap(lev + far, n_lev), way)
-    gh_copy = pltpu.make_async_copy(gho, gh_out, out_sem.at[1])
-    gh_copy.start()
+    own_copies[1].wait()
 
     for c in sends:
         c.wait_send()
@@ -562,8 +571,57 @@
     ac_sent()
     for j in range(1, n_lev):
         z_make(j).wait_send()
-    gw_copy.wait()
-    gh_copy.wait()
+
+
+def finish(
+    dims, agr_ref, wg_ref, ext_ref, gb_ref,
+    gh_out, gw_out, gg_out, gbeta_out, gb_out,
+    agr, gho, gw_v, in_sem, out_sem, gw_sem,
+):
+    nn, rows, parts = dims
+    step = nn // parts
+
+    def fetch(k):
+        at = pl.ds(k * step, step)
+        return pltpu.make_async_copy(agr_ref.at[:, at], agr.at[:, at], in_sem.at[k])
+
+    def store(k):
+        at = pl.ds(k * step * rows, step * rows)
+        return pltpu.make_async_copy(gho.at[at], gh_out.at[at], out_sem.at[k])
+
+    def fetch_gw(k):
+        return pltpu.make_async_copy(wg_ref.at[k], gw_v.at[k], gw_sem.at[0, k])
+
+    def store_gw(k):
+        return pltpu.make_async_copy(gw_v.at[k], gw_out.at[k], gw_sem.at[1, k])
+
+    for k in range(parts):
+        fetch(k).start()
+    for k in range(2):
+        fetch_gw(k).start()
+    full = ext_ref[...].reshape(nn, nn + LANES)
+    gg_out[...] = full[:, :nn]
+    eye = lax.broadcasted_iota(jnp.int32, (nn, nn), 0) == lax.broadcasted_iota(
+        jnp.int32, (nn, nn), 1
+    )
+    gbeta_out[...] = jnp.sum(
+        jnp.where(eye, full[:, nn + LANES - 1 : nn + LANES], 0.0), axis=0, keepdims=True
+    )
+    gb_out[...] = gb_ref[...]
+    for k in range(parts):
+        fetch(k).wait()
+        for i in range(rows):
+            gho[pl.ds(k * step * rows + i, step, stride=rows), :] = agr[
+                i, k * step : (k + 1) * step, :
+            ].astype(F32)
+        store(k).start()
+        if k >= parts - 2:
+            fetch_gw(k - parts + 2).wait()
+            store_gw(k - parts + 2).start()
+    for k in range(parts):
+        store(k).wait()
+    for k in range(2):
+        store_gw(k).wait()
 
 
 def local(sizes, target, hidden, weight, bias, gamma, beta):
@@ -592,38 +650,37 @@
         V((nn, cells), F32), V((nn, cells), F32), V((nn, cells), BF16), V((nn, cells), BF16),
         V((nn, 3 * nn), BF16), V((nn, 3 * nn), BF16), V((nn, taps * chans), BF16),
         V((3 * nn, rpad * cols), BF16), V((2, 4 * chans, rpad * cols), BF16),
-        V((rpad * cols, cols), BF16), V((rpad, 2 * cols, 2 * cols), BF16),
-        V((2, nn, cols), BF16), V((2, nn, cols), BF16), V((nn, cols), BF16),
-        V((2, nn, cols), BF16), V((2, 2 * chans, cols), BF16), V((2, 2 * chans, cols), BF16),
+        V((cells, cols), BF16), V((nn, cols), BF16), V((6, nn, cols), BF16),
+        V((2, 2 * chans, cols), BF16), V((2, 2 * chans, cols), BF16),
+        V((2, 2 * chans, cols), BF16),
         V((2, n_chip, half, nn), F32), V((n_chip, half, nn), F32), V((n_chip, half, nn), BF16),
-        V((n_chip, half, nn), BF16), V((2, n_chip, half, nn), F32),
+        V((n_chip, half, nn), BF16), V((half, nn), F32),
         V((rows, nn, cols), F32), V((cols, cols), F32), V((nn, cells), BF16), V((nn, cells), BF16),
         V((nn, wide), F32), V((nn // 2, wide), F32), V((n_chip, share, wide), F32),
         V((n_chip, share, wide), F32), V((n_lev, share, wide), F32),
-        V((2, n_chip, share, wide), F32),
+        V((share, wide), F32),
         V((2, far + 1, 2, nn, cols), F32), V((2, far + 1, 2, nn, cols), F32),
-        V((rows, nn, cols), BF16), V((nn * rows, cols), F32),
-        D((4,)), D((2,)),
-        D((2,)), D((2,)), D((2,)), D((2,)), D((2,)), D((2,)), D((2,)), D((2,)),
+        V((2, nn, cols), BF16),
+        D((4,)), D((3,)),
+        D((2,)), D((2,)), D((6,)), D((6,)), D((2,)), D((2,)), D((6,)), D((6,)),
         D, D, D((n_chip,)), D((n_chip,)), D((n_chip,)), D((n_chip,)), D, D,
         D, D, D((n_chip,)), D((n_chip,)), D((n_lev,)), D((n_lev,)), D((n_chip,)), D((n_chip,)),
         D, D,
-        D((2, far + 1, 2)), D((2, far + 1, 2)), D((2, far + 1, 2)), D((2, far + 1, 2)),
+        D((2, far + 1, 2)), D((2, far + 1, 2)), D((2, far + 1)), D((2, far + 1)),
     ]
     hbm = pl.BlockSpec(memory_space=pl.ANY)
     vmem = pl.BlockSpec(memory_space=pltpu.VMEM)
     smem = pl.BlockSpec(memory_space=pltpu.SMEM)
-    gh, gw, gb, gg, gbeta = pl.pallas_call(
+    agr, wg, ext, gb = pl.pallas_call(
         functools.partial(kernel, dims),
         out_shape=(
-            jax.ShapeDtypeStruct((nn * rows, cols), F32),
+            jax.ShapeDtypeStruct((rows, nn, cols), BF16),
             jax.ShapeDtypeStruct((2, n_chip, half, nn), F32),
+            jax.ShapeDtypeStruct((2, n_chip, share, wide), F32),
             jax.ShapeDtypeStruct((1, chans), F32),
-            jax.ShapeDtypeStruct((nn, nn), F32),
-            jax.ShapeDtypeStruct((1, nn), F32),
         ),
         in_specs=[smem, hbm, hbm, hbm, vmem, hbm, vmem],
-        out_specs=(hbm, hbm, vmem, vmem, vmem),
+        out_specs=(hbm, hbm, hbm, vmem),
         scratch_shapes=scratch,
         compiler_params=pltpu.CompilerParams(
             collective_id=0, has_side_effects=True, vmem_limit_bytes=60 * 2**20
@@ -632,6 +689,24 @@
         jnp.asarray(area.reshape(-1)), hidden, target, weight, bias.reshape(1, chans),
         gamma, beta.reshape(1, nn),
     )
+    parts = 4
+    gh, gw, gg, gbeta, gb = pl.pallas_call(
+        functools.partial(finish, (nn, rows, parts)),
+        out_shape=(
+            jax.ShapeDtypeStruct((nn * rows, cols), F32),
+            jax.ShapeDtypeStruct((2, n_chip, half, nn), F32),
+            jax.ShapeDtypeStruct((nn, nn), F32),
+            jax.ShapeDtypeStruct((1, nn), F32),
+            jax.ShapeDtypeStruct((1, chans), F32),
+        ),
+        in_specs=[hbm, hbm, vmem, vmem],
+        out_specs=(hbm, hbm, vmem, vmem, vmem),
+        scratch_shapes=[
+            V((rows, nn, cols), BF16), V((nn * rows, cols), F32), V((2, n_chip, half, nn), F32),
+            D((parts,)), D((parts,)), D((2, 2)),
+        ],
+        compiler_params=pltpu.CompilerParams(vmem_limit_bytes=60 * 2**20),
+    )(agr, wg, ext, gb)
     return (
         gh.reshape(nn, rows, cols), gw.reshape(taps, chans, nn), gb.reshape(chans), gg,
         gbeta.reshape(nn),

time: 97.4 us -> 91.3 us (0.937)
  the two profiles are of different devices: /device:TPU:6 before, /device:TPU:1 now
where the time goes in v2:
time: 91.3 us; the launch traced here: 91.1 us
  Pallas kernels  90.5 us (99%)
    pallas_call x1, Pallas kernels, local(): pl.pallas_call(functools.partial(kernel, dims), out_shape=(jax.ShapeDtype...  85.5 us
    pallas_call x1, Pallas kernels, local(): pl.pallas_call(functools.partial(finish, (nn, rows, parts)), out_shape=(j...  5 us

profile of v2, /device:TPU:1, one launch (start us, length us, event | category | flops | bytes accessed | tf_op | source)
XLA Modules:
  0.0 91.1 jit_solution(15139095316891350916)
XLA Ops:
  0.6 85.5 %shard_map.110 = (bf16[16,256,128]{2,1,0:T(8,128)(2,1)}, f32[2,16,48,256]{3,2,1,0:T(8,128)}, f32[2,16,8,384]{3,2,1,0:T(8,128)}, f32[1,96]{1,0:T(1,128)}) custom-call(f32[128]{0:T(128)} %constant.2.clone.area_ref, bf16[256,16,128]{2,1,0:T(8,128)(2,1)} %hidden_ref.1, bf16[4,96,16,128]{3,2,1,0:T(8,128)(2,1)} %target_ref.1, bf16[16,96,256]{2,1,0:T(8,128)(2,1)} %weight_ref.1, ...), custom_call_target="tpu_custom_call" | custom-call | tf_op jit(solution)/shard_map/pallas_call | solution.py:674
  86.1 5.0 %shard_map.111 = (f32[4096,128]{1,0:T(8,128)}, f32[2,16,48,256]{3,2,1,0:T(8,128)}, f32[256,256]{1,0:T(8,128)}, f32[1,256]{1,0:T(1,128)}, f32[1,96]{1,0:T(1,128)}) custom-call(bf16[16,256,128]{2,1,0:T(8,128)(2,1)} %get-tuple-element.14.agr_ref, f32[2,16,48,256]{3,2,1,0:T(8,128)} %get-tuple-element.15.wg_ref, f32[2,16,8,384]{3,2,1,0:T(8,128)} %get-tuple-element.16.ext_ref, ...), custom_call_target="tpu_custom_call" | custom-call | tf_op jit(solution)/shard_map/pallas_call | solution.py:693

commit v3 on v2

--- a/solution.py
+++ b/solution.py
@@ -38,11 +38,11 @@
     gh_out, gw_out, ext_out, gb_out,
     hid_v, tgt_v, w_v, gamma_v,
     hf, tf, hx, root_s, hr_s, sqh, sql, g3, gt3, wt,
-    us, gs, sel, eu_send, eu_recv, eg_send, eg_recv, eg_corner,
+    us, gs, sel, hh_send, hh_recv, eu_send, eu_recv, eg_send, eg_recv, eg_corner,
     dw, dwp, rsb, rsr, wown,
     gu, bacc, mh, ml, ext, extp, exts, extr, extz, eown,
-    abuf, arecv, ghown,
-    in_sem, out_sem,
+    abuf, arecv, agr,
+    in_sem, out_sem, put_sem,
     row_ss, row_rs, eu_ss, eu_rs, grow_ss, grow_rs, eg_ss, eg_rs,
     pw_ss, pw_rs, rb_ss, rb_rs, ab_ss, ab_rs, pg_ss, pg_rs,
     pe_ss, pe_rs, rc_ss, rc_rs, z_ss, z_rs, ac_ss, ac_rs, pc_ss, pc_rs,
@@ -117,22 +117,32 @@
     inputs[0].wait()
     hf[...] = hid_v[...].astype(F32).reshape(nn * rows, LANES)
 
+    mid = slice(nn, 2 * nn)
+
     def spread(i, c):
-        hx[:, lanes(i + 1)] = hf[pl.ds(i, nn, stride=rows), :]
-        return c
-
-    lax.fori_loop(0, rows, spread, 0)
+        x = hf[pl.ds(i, nn, stride=rows), :]
+        hx[:, lanes(i + 1)] = x
+        us[mid, lanes(i + 1)] = x.astype(BF16)
+        return c
+
+    lax.fori_loop(0, rows, spread, 0, unroll=2)
+    hh_send[0] = us[mid, lanes(1)]
+    hh_send[1] = us[mid, lanes(rows)]
+
     def make_sel(r, c):
-        k = lax.broadcasted_iota(jnp.int32, (LANES, LANES), 0)
-        e = lax.broadcasted_iota(jnp.int32, (LANES, LANES), 1)
+        e = lax.broadcasted_iota(jnp.int32, (64, LANES), 0)
+        k = lax.broadcasted_iota(jnp.int32, (64, LANES), 1)
         last, first = k == LANES - 1, k == 0
         hit = (last & (e == r)) | (first & (e == 32 + r))
         hit = hit | ((r == rows) & ((last & (e == 0)) | (first & (e == 32))))
         hit = hit | ((r == 1) & ((last & (e == rows + 1)) | (first & (e == 33 + rows))))
-        sel[lanes(r - 1), :] = jnp.where(hit, 1.0, 0.0).astype(BF16)
+        sel[:, lanes(r - 1)] = jnp.where(hit, 1.0, 0.0).astype(BF16)
         return c
 
     lax.fori_loop(1, rows + 1, make_sel, 0)
+    columns = dot_nt(sel[...], us[mid, lanes(1, rows)]).astype(BF16)
+    eu_send[0] = columns[:32]
+    eu_send[1] = columns[32:]
 
     inputs[1].wait()
     gamma = gamma_v[...]
@@ -148,6 +158,23 @@
         jnp.int32, (chans, chans), 1
     )
     bias_col = jnp.sum(jnp.where(eye_c, bias_ref[...], 0.0), axis=1, keepdims=True)
+
+    pl.semaphore_wait(barrier, 6 + (n_chip - 1) + (n_lev - 1))
+
+    sends = []
+
+    def go(copy):
+        copy.start()
+        sends.append(copy)
+        return copy
+
+    eu_copies = [
+        go(remote(eu_send.at[i % 2], eu_recv.at[i], eu_ss.at[i], eu_rs.at[i], device))
+        for i, device in enumerate((east, west, southeast, southwest, northeast, northwest))
+    ] + [
+        go(remote(hh_send.at[0], hh_recv.at[1], row_ss.at[0], row_rs.at[0], north)),
+        go(remote(hh_send.at[1], hh_recv.at[0], row_ss.at[1], row_rs.at[1], south)),
+    ]
 
     def root_of(x):
         s_hi, s_lo = split(x * x)
@@ -169,27 +196,6 @@
 
     north_in = jnp.where(lat > 0, 1.0, 0.0).astype(F32)
     south_in = jnp.where(lat < n_lat - 1, 1.0, 0.0).astype(F32)
-    eu_send[...] = dot(us[nn : 2 * nn, lanes(1, rows)], sel[...]).astype(BF16)
-
-    pl.semaphore_wait(barrier, 6 + (n_chip - 1) + (n_lev - 1))
-
-    sends = []
-
-    def go(copy):
-        copy.start()
-        sends.append(copy)
-        return copy
-
-    mid = slice(nn, 2 * nn)
-    eu_copies = [
-        go(remote(us.at[mid, lanes(1)], us.at[mid, lanes(rpad - 1)],
-                  row_ss.at[0], row_rs.at[0], north)),
-        go(remote(us.at[mid, lanes(rows)], us.at[mid, lanes(0)],
-                  row_ss.at[1], row_rs.at[1], south)),
-    ] + [
-        go(remote(eu_send, eu_recv.at[i], eu_ss.at[i], eu_rs.at[i], device))
-        for i, device in enumerate((east, west, southeast, southwest, northeast, northwest))
-    ]
 
     inputs[3].wait()
     order = []
@@ -219,14 +225,22 @@
 
     for c in eu_copies:
         c.wait_recv()
-    us[mid, lanes(0)] = (us[mid, lanes(0)].astype(F32) * north_in).astype(BF16)
-    us[mid, lanes(rpad - 1)] = (us[mid, lanes(rpad - 1)].astype(F32) * south_in).astype(BF16)
-    lane = lax.broadcasted_iota(jnp.int32, (nn, LANES), 1)
-    eu_mix = jnp.where(lane < 32, eu_recv[0].astype(F32), eu_recv[1].astype(F32))
-    for i, at, keep in (
-        (2, 0, north_in), (3, 32, north_in), (4, rows + 1, south_in), (5, rows + 33, south_in)
-    ):
-        eu_mix = jnp.where(lane == at, eu_recv[i].astype(F32) * keep, eu_mix)
+    row = lax.broadcasted_iota(jnp.int32, (32, nn), 0)
+
+    def side(i):
+        x = eu_recv[i].astype(F32)
+        x = jnp.where(row == 0, eu_recv[i + 2].astype(F32) * north_in, x)
+        return jnp.where(row == rows + 1, eu_recv[i + 4].astype(F32) * south_in, x)
+
+    columns = jnp.concatenate([side(0), side(1), jnp.zeros((64, nn), F32)], axis=0).T
+    x = jnp.concatenate(
+        [hh_recv[0].astype(F32) * north_in, hh_recv[1].astype(F32) * south_in, columns], axis=1
+    )
+    root, _, _ = root_of(x)
+    edge = (x * root).astype(BF16)
+    us[mid, lanes(0)] = edge[:, :LANES]
+    us[mid, lanes(rpad - 1)] = edge[:, LANES : 2 * LANES]
+    eu_mix = edge[:, 2 * LANES :].astype(F32)
 
     def from_west(x, e, r):
         at = lax.broadcasted_iota(jnp.int32, x.shape, 1)
@@ -234,13 +248,13 @@
 
     def from_east(x, e, r):
         at = lax.broadcasted_iota(jnp.int32, x.shape, 1)
-        edge = pltpu.roll(e, LANES - 33 - r, 1)
+        edge = pltpu.roll(e, LANES - 1 - r, 1)
         return jnp.where(at == LANES - 1, edge, pltpu.roll(x, LANES - 1, 1))
 
     def shift_u(r, c):
         x = us[mid, lanes(r)].astype(F32)
         us[:nn, lanes(r)] = from_west(x, eu_mix, r).astype(BF16)
-        us[2 * nn :, lanes(r)] = from_east(x, eu_mix, r).astype(BF16)
+        us[2 * nn :, lanes(r)] = from_east(x, eu_mix, 32 + r).astype(BF16)
         return c
 
     lax.fori_loop(0, rpad, shift_u, 0, unroll=3)
@@ -273,37 +287,39 @@
                   grow_ss.at[1], grow_rs.at[1], south)),
     ]
     lax.fori_loop(2, rows // 2, recon_tile, 0, unroll=2)
+    pad = LANES - chans
     for p in range(2):
-        eg_send[p] = dot(gs[p, : 2 * chans, lanes(1, rows)], sel[...]).astype(BF16)
-    east_part, west_part = slice(0, chans), slice(chans, 2 * chans)
+        for q in range(2):
+            block = gs[p, q * (chans - pad) : q * (chans - pad) + LANES, lanes(1, rows)]
+            eg_send[q, p] = dot_nt(sel[32 * (1 - q) : 32 * (2 - q), :], block).astype(BF16)
     eg_copies = [
         go(remote(src, dst, eg_ss.at[i], eg_rs.at[i], device))
         for i, (src, dst, device) in enumerate((
-            (eg_send.at[:, east_part], eg_recv.at[:, east_part], west),
-            (eg_send.at[:, west_part], eg_recv.at[:, west_part], east),
-            (eg_send.at[0, east_part], eg_corner.at[0, east_part], northwest),
-            (eg_send.at[0, west_part], eg_corner.at[0, west_part], northeast),
-            (eg_send.at[1, east_part], eg_corner.at[1, east_part], southwest),
-            (eg_send.at[1, west_part], eg_corner.at[1, west_part], southeast),
+            (eg_send.at[0], eg_recv.at[0], west),
+            (eg_send.at[1], eg_recv.at[1], east),
+            (eg_send.at[0, 0], eg_corner.at[0, 0], northwest),
+            (eg_send.at[1, 0], eg_corner.at[1, 0], northeast),
+            (eg_send.at[0, 1], eg_corner.at[0, 1], southwest),
+            (eg_send.at[1, 1], eg_corner.at[1, 1], southeast),
         ))
     ]
 
     per_tap = chans // half
 
-    def grad_taps(slot, p):
-        for q in range(2):
-            for a in range(2):
-                y = dot_nt(
-                    gs[p, q * chans : (q + 1) * chans, lanes(1, rows)],
-                    us[q * nn : (q + 2) * nn, lanes(p + a, rows)],
-                )
-                for b in range(2):
-                    for k in range(per_tap):
-                        dw[slot, (4 * q + 2 * a + b) * per_tap + k] = y[
-                            k * half : (k + 1) * half, b * nn : (b + 1) * nn
-                        ]
-
-    grad_taps(0, 1 - core)
+    def grad_taps(slot, p, q):
+        for a in range(2):
+            y = dot_nt(
+                gs[p, q * chans : (q + 1) * chans, lanes(1, rows)],
+                us[q * nn : (q + 2) * nn, lanes(p + a, rows)],
+            )
+            for b in range(2):
+                for k in range(per_tap):
+                    dw[slot, (4 * q + 2 * a + b) * per_tap + k] = y[
+                        k * half : (k + 1) * half, b * nn : (b + 1) * nn
+                    ]
+
+    grad_taps(0, 1 - core, 0)
+    grad_taps(0, 1 - core, 1)
     pw = go(remote(dw.at[0], dwp, pw_ss, pw_rs, pair))
 
     for c in grow_copies + eg_copies:
@@ -314,23 +330,25 @@
     gs[1, : 2 * chans, lanes(0)] = (
         gs[1, : 2 * chans, lanes(0)].astype(F32) * north_in
     ).astype(BF16)
-    lane = lax.broadcasted_iota(jnp.int32, (2 * chans, LANES), 1)
-    eg_mix = []
+    row = lax.broadcasted_iota(jnp.int32, (32, LANES), 0)
+    eg_mix = {}
     for p, at, keep in ((0, rows + 1, south_in), (1, 0, north_in)):
-        corner = eg_corner[p].astype(F32) * keep
-        eg_mix.append(
-            jnp.where((lane == at) | (lane == at + 32), corner, eg_recv[p].astype(F32))
-        )
+        for q in range(2):
+            x = jnp.where(
+                row == at, eg_corner[q, p].astype(F32) * keep, eg_recv[q, p].astype(F32)
+            )
+            x = jnp.concatenate([x, jnp.zeros((LANES - 32, LANES), F32)], axis=0).T
+            eg_mix[p, q] = x[q * pad : q * pad + chans]
 
     def shift_g(r, c):
         for p in range(2):
             rr = r + 1 - p
             x = gs[p, : 2 * chans, lanes(rr)].astype(F32)
             gs[p, 2 * chans : 3 * chans, lanes(rr)] = from_east(
-                x[:chans], eg_mix[p][:chans], rr
+                x[:chans], eg_mix[p, 0], rr
             ).astype(BF16)
             gs[p, 3 * chans :, lanes(rr)] = from_west(
-                x[chans:], eg_mix[p][chans:], rr
+                x[chans:], eg_mix[p, 1], rr
             ).astype(BF16)
         return c
 
@@ -351,20 +369,41 @@
             gu[2 * k + 1] = y[:, (2 * i + 1) * LANES : (2 * i + 2) * LANES]
 
     far = n_lev // 2
+    cuts = 2
+    piece = nn // cuts
     rs_copies = {}
 
     def rs_send(way, s, h, first):
         owner = wrap(lev + (far + 1 - s if way else s - far - 1), n_lev)
-        row = 2 * owner + h
-        if first:
-            src = gu.at[row]
-        else:
-            rs_copies[way, s - 1, h].wait_recv()
-            abuf[way, s, h] = gu[row] + arecv[way, s - 1, h]
-            src = abuf.at[way, s, h]
-        rs_copies[way, s, h] = go(
-            remote(src, arecv.at[way, s, h], a_ss.at[way, s, h], a_rs.at[way, s, h],
-                   above if way else below)
+        for k in range(cuts):
+            at = pl.ds(k * piece, piece)
+            src = gu.at[2 * owner + h, at]
+            if not first:
+                rs_copies[way, s - 1, h, k].wait_recv()
+                abuf[way, s, h, at] = gu[2 * owner + h, at] + arecv[way, s - 1, h, at]
+                src = abuf.at[way, s, h, at]
+            rs_copies[way, s, h, k] = go(
+                remote(src, arecv.at[way, s, h, at], a_ss.at[way, s, h, k],
+                       a_rs.at[way, s, h, k], above if way else below)
+            )
+
+    def over_chips(make):
+        def start(j, c):
+            make(j).start()
+            return c
+
+        def arrive(j, c):
+            make(j).wait_recv()
+            return c
+
+        def sent(j, c):
+            make(j).wait_send()
+            return c
+
+        lax.fori_loop(1, n_chip, start, 0)
+        return (
+            lambda: lax.fori_loop(1, n_chip, arrive, 0),
+            lambda: lax.fori_loop(1, n_chip, sent, 0),
         )
 
     grad_rows(wrap(lev + far, n_lev))
@@ -373,46 +412,7 @@
     grad_rows(wrap(lev + far - 1, n_lev), wrap(lev + far + 1, n_lev))
     rs_send(1, 2, 0, True)
     rs_send(0, 2, 1, True)
-    grad_taps(1, core)
-
-    def over_chips(make):
-        def start(j, c):
-            make(j).start()
-            return c
-
-        def arrive(j, c):
-            make(j).wait_recv()
-            return c
-
-        def sent(j, c):
-            make(j).wait_send()
-            return c
-
-        lax.fori_loop(1, n_chip, start, 0)
-        return (
-            lambda: lax.fori_loop(1, n_chip, arrive, 0),
-            lambda: lax.fori_loop(1, n_chip, sent, 0),
-        )
-
-    def rb_make(j):
-        k = wrap(chip + j, n_chip)
-        return remote(rsb.at[k], rsr.at[j], rb_ss.at[j], rb_rs.at[j], at_chip(k))
-
-    rs_send(0, 2, 0, False)
-    rs_send(1, 2, 1, False)
     grad_rows(wrap(lev + far - 2, n_lev), wrap(lev + far + 2, n_lev))
-    pw.wait_recv()
-
-    def join(k, c):
-        dw[1, k] = dw[1, k] + dwp[k]
-        rsb[k] = dw[1, k].astype(BF16)
-        return c
-
-    lax.fori_loop(0, n_chip, join, 0)
-    rb_arrive, rb_sent = over_chips(rb_make)
-
-    for way, h in ((0, 1), (1, 0), (0, 0), (1, 1)):
-        rs_send(way, 3, h, False)
     grad_rows(wrap(lev + 1, n_lev), wrap(lev + n_lev - 1, n_lev))
     grad_rows(lev)
 
@@ -437,25 +437,8 @@
     others = pl.multiple_of((1 - core) * (nn // 2), nn // 2)
     pe = go(remote(ext.at[pl.ds(others, nn // 2)], extp, pe_ss, pe_rs, pair))
 
-    for way, h in ((0, 1), (1, 0), (0, 0), (1, 1)):
-        rs_send(way, 4, h, False)
-
-    rb_arrive()
-
-    def add_taps(j, acc):
-        return acc + rsr[j].astype(F32)
-
-    wown[...] = lax.fori_loop(1, n_chip, add_taps, dw[1, chip]) * (1.0 / total_cells)
-    own_copies = [pltpu.make_async_copy(wown, gw_out.at[core, chip], out_sem.at[0])]
-    own_copies[0].start()
-
-    def ab_make(j):
-        k = wrap(chip + j, n_chip)
-        return remote(
-            wown, gw_out.at[core, chip], ab_ss.at[j], ab_rs.at[j], at_chip(k)
-        )
-
-    ab_arrive, ab_sent = over_chips(ab_make)
+    rs_send(0, 2, 0, False)
+    rs_send(1, 2, 1, False)
 
     pe.wait_recv()
 
@@ -472,43 +455,26 @@
         return remote(exts.at[k], extr.at[chip], rc_ss.at[j], rc_rs.at[j], at_chip(k))
 
     rc_arrive, rc_sent = over_chips(rc_make)
-
-    for way in range(2):
-        for h in range(2):
-            rs_copies[way, 4, h].wait_recv()
-    g = jnp.concatenate(
-        [gu[2 * lev + h] + (arecv[0, 4, h] + arecv[1, 4, h]) for h in range(2)], axis=1
-    )
-    at = lanes(2 * lev, 2)
-    m_hi, m_lo = split(g * hr_s[:, at])
-    back = dot(gt3[...], jnp.concatenate([m_hi, m_hi, m_lo], axis=0))
-    gh = (g * root_s[:, at] + 2.0 * hx[:, lanes(2 * lev + 1, 2)] * back).astype(BF16)
-    ghown[0] = gh[:, :LANES]
-    ghown[1] = gh[:, LANES:]
-    own_copies.append(
-        pltpu.make_async_copy(ghown, gh_out.at[pl.ds(2 * lev, 2)], out_sem.at[1])
-    )
-    own_copies[1].start()
-
-    ag_copies = {}
-
-    def ag_send(way, hops, origin, kind, src=None):
-        step = hops if way else -hops
-        owner = wrap(lev - origin if way else lev + origin, n_lev)
-        if kind == 2:
-            rows_of = pl.ds(2 * owner, 2)
-        else:
-            rows_of = pl.ds(2 * owner + kind, 1)
-        block = gh_out.at[rows_of]
-        ag_copies[way, hops + origin] = go(
-            remote(block if src is None else src, block, g_ss.at[way, hops + origin],
-                   g_rs.at[way, hops + origin], (lat, lon, wrap(lev + step, n_lev)))
-        )
-
-    for way in range(2):
-        ag_send(way, 1, 0, 2, ghown)
-    for way in range(2):
-        ag_send(way, 2, 0, 2, ghown)
+    grad_taps(1, core, 0)
+    rs_send(1, 3, 0, False)
+    rs_send(0, 3, 1, False)
+    grad_taps(1, core, 1)
+    pw.wait_recv()
+
+    def join(k, c):
+        dw[1, k] = dw[1, k] + dwp[k]
+        rsb[k] = dw[1, k].astype(BF16)
+        return c
+
+    lax.fori_loop(0, n_chip, join, 0)
+
+    def rb_make(j):
+        k = wrap(chip + j, n_chip)
+        return remote(rsb.at[k], rsr.at[j], rb_ss.at[j], rb_rs.at[j], at_chip(k))
+
+    rb_arrive, rb_sent = over_chips(rb_make)
+    rs_send(0, 3, 0, False)
+    rs_send(1, 3, 1, False)
 
     rc_arrive()
 
@@ -527,17 +493,25 @@
     for j in range(1, n_lev):
         z_make(j).start()
 
-    for way in range(2):
-        ag_copies[way, 1].wait_recv()
-        ag_send(way, 2, 1, 2)
-
-    ab_arrive()
-    own_copies[0].wait()
-    pg = go(remote(gw_out.at[core], gw_out.at[core], pg_ss, pg_rs, pair))
-
-    for way in range(2):
-        ag_copies[way, 2].wait_recv()
-        ag_send(way, 2, 2, way)
+    rs_send(1, 4, 0, False)
+    rs_send(0, 4, 1, False)
+
+    rb_arrive()
+
+    def add_taps(j, acc):
+        return acc + rsr[j].astype(F32)
+
+    wown[...] = lax.fori_loop(1, n_chip, add_taps, dw[1, chip]) * (1.0 / total_cells)
+    w_copy = pltpu.make_async_copy(wown, gw_out.at[core, chip], out_sem.at[0])
+    w_copy.start()
+
+    def ab_make(j):
+        k = wrap(chip + j, n_chip)
+        return remote(wown, gw_out.at[core, chip], ab_ss.at[j], ab_rs.at[j], at_chip(k))
+
+    ab_arrive, ab_sent = over_chips(ab_make)
+    rs_send(0, 4, 0, False)
+    rs_send(1, 4, 1, False)
 
     for j in range(1, n_lev):
         z_make(j).wait_recv()
@@ -545,23 +519,79 @@
     for k in range(1, n_lev):
         whole = whole + extz[k]
     eown[...] = whole * (1.0 / total_cells)
-    own_copies.append(pltpu.make_async_copy(eown, ext_out.at[core, chip], out_sem.at[2]))
-    own_copies[2].start()
+    e_copy = pltpu.make_async_copy(eown, ext_out.at[core, chip], out_sem.at[1])
+    e_copy.start()
 
     def ac_make(j):
         k = wrap(chip + j, n_chip)
         return remote(eown, ext_out.at[core, chip], ac_ss.at[j], ac_rs.at[j], at_chip(k))
 
     ac_arrive, ac_sent = over_chips(ac_make)
+
+    for way, h in ((1, 0), (0, 1), (0, 0), (1, 1)):
+        for k in range(cuts):
+            rs_copies[way, far, h, k].wait_recv()
+    g = jnp.concatenate(
+        [gu[2 * lev + h] + (arecv[0, far, h] + arecv[1, far, h]) for h in range(2)], axis=1
+    )
+    at = lanes(2 * lev, 2)
+    m_hi, m_lo = split(g * hr_s[:, at])
+    back = dot(gt3[...], jnp.concatenate([m_hi, m_hi, m_lo], axis=0))
+    gh = (g * root_s[:, at] + 2.0 * hx[:, lanes(2 * lev + 1, 2)] * back).astype(BF16)
+    agr[2 * lev] = gh[:, :LANES]
+    agr[2 * lev + 1] = gh[:, LANES:]
+
+    ag_copies = {}
+
+    def ag_send(s):
+        for h in range(2):
+            for way in range(2):
+                if s == far and h != way:
+                    continue
+                owner = wrap(lev + (1 - s if way else s - 1), n_lev)
+                for k in range(cuts):
+                    if s > 1:
+                        ag_copies[way, s - 1, h, k].wait_recv()
+                    block = agr.at[2 * owner + h, pl.ds(k * piece, piece)]
+                    ag_copies[way, s, h, k] = go(
+                        remote(block, block, g_ss.at[way, s, h, k], g_rs.at[way, s, h, k],
+                               above if way else below)
+                    )
+
+    put_copies = []
+
+    def put(i, owner):
+        block = pl.ds(2 * owner, 2)
+        copy = pltpu.make_async_copy(agr.at[block], gh_out.at[block], put_sem.at[i])
+        copy.start()
+        put_copies.append(copy)
+
+    ag_send(1)
+    put(0, lev)
     ac_arrive()
-    own_copies[2].wait()
+    e_copy.wait()
     pc = go(remote(ext_out.at[core], ext_out.at[core], pc_ss, pc_rs, pair))
+    ag_send(2)
+    put(1, wrap(lev + 1, n_lev))
+    put(2, wrap(lev - 1, n_lev))
+    ab_arrive()
+    w_copy.wait()
+    pg = go(remote(gw_out.at[core], gw_out.at[core], pg_ss, pg_rs, pair))
+    ag_send(3)
+    put(3, wrap(lev + 2, n_lev))
+    put(4, wrap(lev - 2, n_lev))
+    ag_send(4)
+    for way in range(2):
+        for k in range(cuts):
+            ag_copies[way, far - 1, 1 - way, k].wait_recv()
+    put(5, wrap(lev + 3, n_lev))
+    put(6, wrap(lev - 3, n_lev))
+    pc.wait_recv()
     pg.wait_recv()
     for way in range(2):
-        ag_copies[way, 3].wait_recv()
-        ag_copies[way, 4].wait_recv()
-    pc.wait_recv()
-    own_copies[1].wait()
+        for k in range(cuts):
+            ag_copies[way, far, way, k].wait_recv()
+    put(7, wrap(lev + far, n_lev))
 
     for c in sends:
         c.wait_send()
@@ -571,12 +601,14 @@
     ac_sent()
     for j in range(1, n_lev):
         z_make(j).wait_send()
+    for c in put_copies:
+        c.wait()
 
 
 def finish(
     dims, agr_ref, wg_ref, ext_ref, gb_ref,
     gh_out, gw_out, gg_out, gbeta_out, gb_out,
-    agr, gho, gw_v, in_sem, out_sem, gw_sem,
+    agr, gho, gw_v, ext_v, gg_v, in_sem, out_sem, gw_sem, ext_sem,
 ):
     nn, rows, parts = dims
     step = nn // parts
@@ -595,19 +627,17 @@
     def store_gw(k):
         return pltpu.make_async_copy(gw_v.at[k], gw_out.at[k], gw_sem.at[1, k])
 
+    fetch_ext = pltpu.make_async_copy(ext_ref, ext_v, ext_sem.at[0])
+    store_gg = pltpu.make_async_copy(gg_v, gg_out, ext_sem.at[1])
     for k in range(parts):
         fetch(k).start()
+    fetch_ext.start()
     for k in range(2):
         fetch_gw(k).start()
-    full = ext_ref[...].reshape(nn, nn + LANES)
-    gg_out[...] = full[:, :nn]
+    gb_out[...] = gb_ref[...]
     eye = lax.broadcasted_iota(jnp.int32, (nn, nn), 0) == lax.broadcasted_iota(
         jnp.int32, (nn, nn), 1
     )
-    gbeta_out[...] = jnp.sum(
-        jnp.where(eye, full[:, nn + LANES - 1 : nn + LANES], 0.0), axis=0, keepdims=True
-    )
-    gb_out[...] = gb_ref[...]
     for k in range(parts):
         fetch(k).wait()
         for i in range(rows):
@@ -615,11 +645,19 @@
                 i, k * step : (k + 1) * step, :
             ].astype(F32)
         store(k).start()
-        if k >= parts - 2:
-            fetch_gw(k - parts + 2).wait()
-            store_gw(k - parts + 2).start()
+    fetch_ext.wait()
+    full = ext_v[...].reshape(nn, nn + LANES)
+    gg_v[...] = full[:, :nn]
+    store_gg.start()
+    gbeta_out[...] = jnp.sum(
+        jnp.where(eye, full[:, nn + LANES - 1 : nn + LANES], 0.0), axis=0, keepdims=True
+    )
+    for k in range(2):
+        fetch_gw(k).wait()
+        store_gw(k).start()
     for k in range(parts):
         store(k).wait()
+    store_gg.wait()
     for k in range(2):
         store_gw(k).wait()
 
@@ -650,9 +688,9 @@
         V((nn, cells), F32), V((nn, cells), F32), V((nn, cells), BF16), V((nn, cells), BF16),
         V((nn, 3 * nn), BF16), V((nn, 3 * nn), BF16), V((nn, taps * chans), BF16),
         V((3 * nn, rpad * cols), BF16), V((2, 4 * chans, rpad * cols), BF16),
-        V((cells, cols), BF16), V((nn, cols), BF16), V((6, nn, cols), BF16),
-        V((2, 2 * chans, cols), BF16), V((2, 2 * chans, cols), BF16),
-        V((2, 2 * chans, cols), BF16),
+        V((64, cells), BF16), V((2, nn, cols), BF16), V((2, nn, cols), BF16),
+        V((2, 32, nn), BF16), V((6, 32, nn), BF16),
+        V((2, 2, 32, cols), BF16), V((2, 2, 32, cols), BF16), V((2, 2, 32, cols), BF16),
         V((2, n_chip, half, nn), F32), V((n_chip, half, nn), F32), V((n_chip, half, nn), BF16),
         V((n_chip, half, nn), BF16), V((half, nn), F32),
         V((rows, nn, cols), F32), V((cols, cols), F32), V((nn, cells), BF16), V((nn, cells), BF16),
@@ -660,13 +698,14 @@
         V((n_chip, share, wide), F32), V((n_lev, share, wide), F32),
         V((share, wide), F32),
         V((2, far + 1, 2, nn, cols), F32), V((2, far + 1, 2, nn, cols), F32),
-        V((2, nn, cols), BF16),
-        D((4,)), D((3,)),
+        V((rows, nn, cols), BF16),
+        D((4,)), D((2,)), D((n_lev,)),
         D((2,)), D((2,)), D((6,)), D((6,)), D((2,)), D((2,)), D((6,)), D((6,)),
         D, D, D((n_chip,)), D((n_chip,)), D((n_chip,)), D((n_chip,)), D, D,
         D, D, D((n_chip,)), D((n_chip,)), D((n_lev,)), D((n_lev,)), D((n_chip,)), D((n_chip,)),
         D, D,
-        D((2, far + 1, 2)), D((2, far + 1, 2)), D((2, far + 1)), D((2, far + 1)),
+        D((2, far + 1, 2, 2)), D((2, far + 1, 2, 2)),
+        D((2, far + 1, 2, 2)), D((2, far + 1, 2, 2)),
     ]
     hbm = pl.BlockSpec(memory_space=pl.ANY)
     vmem = pl.BlockSpec(memory_space=pltpu.VMEM)
@@ -699,11 +738,12 @@
             jax.ShapeDtypeStruct((1, nn), F32),
             jax.ShapeDtypeStruct((1, chans), F32),
         ),
-        in_specs=[hbm, hbm, vmem, vmem],
-        out_specs=(hbm, hbm, vmem, vmem, vmem),
+        in_specs=[hbm, hbm, hbm, vmem],
+        out_specs=(hbm, hbm, hbm, vmem, vmem),
         scratch_shapes=[
             V((rows, nn, cols), BF16), V((nn * rows, cols), F32), V((2, n_chip, half, nn), F32),
-            D((parts,)), D((parts,)), D((2, 2)),
+            V((2, n_chip, share, wide), F32), V((nn, nn), F32),
+            D((parts,)), D((parts,)), D((2, 2)), D((2,)),
         ],
         compiler_params=pltpu.CompilerParams(vmem_limit_bytes=60 * 2**20),
     )(agr, wg, ext, gb)

time: 91.3 us -> 83 us (0.909)
  the two profiles are of different devices: /device:TPU:1 before, /device:TPU:6 now
where the time goes in v3:
time: 83 us; the launch traced here: 81.8 us
  Pallas kernels  81.2 us (98%)
    pallas_call x1, Pallas kernels, local(): pl.pallas_call(functools.partial(kernel, dims), out_shape=(jax.ShapeDtype...  76.6 us
    pallas_call x1, Pallas kernels, local(): pl.pallas_call(functools.partial(finish, (nn, rows, parts)), out_shape=(j...  4.63 us

profile of v3, /device:TPU:6, one launch (start us, length us, event | category | flops | bytes accessed | tf_op | source)
XLA Modules:
  0.0 81.8 jit_solution(14071616333912897837)
XLA Ops:
  0.6 76.6 %shard_map.110 = (bf16[16,256,128]{2,1,0:T(8,128)(2,1)}, f32[2,16,48,256]{3,2,1,0:T(8,128)}, f32[2,16,8,384]{3,2,1,0:T(8,128)}, f32[1,96]{1,0:T(1,128)}) custom-call(f32[128]{0:T(128)} %constant.2.clone.area_ref, bf16[256,16,128]{2,1,0:T(8,128)(2,1)} %hidden_ref.1, bf16[4,96,16,128]{3,2,1,0:T(8,128)(2,1)} %target_ref.1, bf16[16,96,256]{2,1,0:T(8,128)(2,1)} %weight_ref.1, ...), custom_call_target="tpu_custom_call" | custom-call | tf_op jit(solution)/shard_map/pallas_call | solution.py:713
  77.2 4.6 %shard_map.111 = (f32[4096,128]{1,0:T(8,128)}, f32[2,16,48,256]{3,2,1,0:T(8,128)}, f32[256,256]{1,0:T(8,128)}, f32[1,256]{1,0:T(1,128)}, f32[1,96]{1,0:T(1,128)}) custom-call(bf16[16,256,128]{2,1,0:T(8,128)(2,1)} %get-tuple-element.14.agr_ref, f32[2,16,48,256]{3,2,1,0:T(8,128)} %get-tuple-element.15.wg_ref, f32[2,16,8,384]{3,2,1,0:T(8,128)} %get-tuple-element.16.ext_ref, ...), custom_call_target="tpu_custom_call" | custom-call | tf_op jit(solution)/shard_map/pallas_call | solution.py:732

commit v4 on v3

--- a/solution.py
+++ b/solution.py
@@ -26,6 +26,26 @@
 
 def dot_nt(a, b):
     return lax.dot_general(a, b, (((1,), (1,)), ((), ())), preferred_element_type=F32)
+
+
+STEPS = 1920.0
+
+
+def pack(x):
+    hi = x.astype(BF16)
+    h = hi.astype(F32)
+    scale = pl.reciprocal(jnp.maximum(jnp.abs(h), 1e-30), approx=True) * STEPS
+    q = jnp.clip(jnp.floor((x - h) * scale + 0.5), -8.0, 7.0)
+    m = x.shape[0] // 2
+    return jnp.concatenate([hi, (16.0 * q[:m] + q[m:]).astype(BF16)], axis=0)
+
+
+def unpack(y):
+    m = y.shape[0] // 3
+    h, p = y[: 2 * m].astype(F32), y[2 * m :].astype(F32)
+    a = jnp.floor((p + 8.0) * 0.0625)
+    q = jnp.concatenate([a, p - 16.0 * a], axis=0)
+    return h + jnp.abs(h) * (q * (1.0 / STEPS))
 
 
 def wrap(index, size):
@@ -144,6 +164,23 @@
     eu_send[0] = columns[:32]
     eu_send[1] = columns[32:]
 
+    pl.semaphore_wait(barrier, 6 + (n_chip - 1) + (n_lev - 1))
+
+    sends = []
+
+    def go(copy):
+        copy.start()
+        sends.append(copy)
+        return copy
+
+    eu_copies = [
+        go(remote(eu_send.at[i % 2], eu_recv.at[i], eu_ss.at[i], eu_rs.at[i], device))
+        for i, device in enumerate((east, west, southeast, southwest, northeast, northwest))
+    ] + [
+        go(remote(hh_send.at[0], hh_recv.at[1], row_ss.at[0], row_rs.at[0], north)),
+        go(remote(hh_send.at[1], hh_recv.at[0], row_ss.at[1], row_rs.at[1], south)),
+    ]
+
     inputs[1].wait()
     gamma = gamma_v[...]
     g_hi, g_lo = split(gamma)
@@ -158,23 +195,6 @@
         jnp.int32, (chans, chans), 1
     )
     bias_col = jnp.sum(jnp.where(eye_c, bias_ref[...], 0.0), axis=1, keepdims=True)
-
-    pl.semaphore_wait(barrier, 6 + (n_chip - 1) + (n_lev - 1))
-
-    sends = []
-
-    def go(copy):
-        copy.start()
-        sends.append(copy)
-        return copy
-
-    eu_copies = [
-        go(remote(eu_send.at[i % 2], eu_recv.at[i], eu_ss.at[i], eu_rs.at[i], device))
-        for i, device in enumerate((east, west, southeast, southwest, northeast, northwest))
-    ] + [
-        go(remote(hh_send.at[0], hh_recv.at[1], row_ss.at[0], row_rs.at[0], north)),
-        go(remote(hh_send.at[1], hh_recv.at[0], row_ss.at[1], row_rs.at[1], south)),
-    ]
 
     def root_of(x):
         s_hi, s_lo = split(x * x)
@@ -321,6 +341,7 @@
     grad_taps(0, 1 - core, 0)
     grad_taps(0, 1 - core, 1)
     pw = go(remote(dw.at[0], dwp, pw_ss, pw_rs, pair))
+    grad_taps(1, core, 0)
 
     for c in grow_copies + eg_copies:
         c.wait_recv()
@@ -377,13 +398,13 @@
         owner = wrap(lev + (far + 1 - s if way else s - far - 1), n_lev)
         for k in range(cuts):
             at = pl.ds(k * piece, piece)
-            src = gu.at[2 * owner + h, at]
+            x = gu[2 * owner + h, at]
             if not first:
                 rs_copies[way, s - 1, h, k].wait_recv()
-                abuf[way, s, h, at] = gu[2 * owner + h, at] + arecv[way, s - 1, h, at]
-                src = abuf.at[way, s, h, at]
+                x = x + unpack(arecv[way, s - 1, h, k])
+            abuf[way, s, h, k] = pack(x)
             rs_copies[way, s, h, k] = go(
-                remote(src, arecv.at[way, s, h, at], a_ss.at[way, s, h, k],
+                remote(abuf.at[way, s, h, k], arecv.at[way, s, h, k], a_ss.at[way, s, h, k],
                        a_rs.at[way, s, h, k], above if way else below)
             )
 
@@ -412,6 +433,21 @@
     grad_rows(wrap(lev + far - 1, n_lev), wrap(lev + far + 1, n_lev))
     rs_send(1, 2, 0, True)
     rs_send(0, 2, 1, True)
+    grad_taps(1, core, 1)
+    pw.wait_recv()
+
+    def join(k, c):
+        dw[1, k] = dw[1, k] + dwp[k]
+        rsb[k] = dw[1, k].astype(BF16)
+        return c
+
+    lax.fori_loop(0, n_chip, join, 0)
+
+    def rb_make(j):
+        k = wrap(chip + j, n_chip)
+        return remote(rsb.at[k], rsr.at[j], rb_ss.at[j], rb_rs.at[j], at_chip(k))
+
+    rb_arrive, rb_sent = over_chips(rb_make)
     grad_rows(wrap(lev + far - 2, n_lev), wrap(lev + far + 2, n_lev))
     grad_rows(wrap(lev + 1, n_lev), wrap(lev + n_lev - 1, n_lev))
     grad_rows(lev)
@@ -455,26 +491,30 @@
         return remote(exts.at[k], extr.at[chip], rc_ss.at[j], rc_rs.at[j], at_chip(k))
 
     rc_arrive, rc_sent = over_chips(rc_make)
-    grad_taps(1, core, 0)
     rs_send(1, 3, 0, False)
     rs_send(0, 3, 1, False)
-    grad_taps(1, core, 1)
-    pw.wait_recv()
-
-    def join(k, c):
-        dw[1, k] = dw[1, k] + dwp[k]
-        rsb[k] = dw[1, k].astype(BF16)
-        return c
-
-    lax.fori_loop(0, n_chip, join, 0)
-
-    def rb_make(j):
-        k = wrap(chip + j, n_chip)
-        return remote(rsb.at[k], rsr.at[j], rb_ss.at[j], rb_rs.at[j], at_chip(k))
-
-    rb_arrive, rb_sent = over_chips(rb_make)
     rs_send(0, 3, 0, False)
     rs_send(1, 3, 1, False)
+
+    rs_send(1, 4, 0, False)
+    rs_send(0, 4, 1, False)
+
+    rb_arrive()
+
+    def add_taps(j, acc):
+        return acc + rsr[j].astype(F32)
+
+    wown[...] = lax.fori_loop(1, n_chip, add_taps, dw[1, chip]) * (1.0 / total_cells)
+    w_copy = pltpu.make_async_copy(wown, gw_out.at[core, chip], out_sem.at[0])
+    w_copy.start()
+
+    def ab_make(j):
+        k = wrap(chip + j, n_chip)
+        return remote(wown, gw_out.at[core, chip], ab_ss.at[j], ab_rs.at[j], at_chip(k))
+
+    ab_arrive, ab_sent = over_chips(ab_make)
+    rs_send(0, 4, 0, False)
+    rs_send(1, 4, 1, False)
 
     rc_arrive()
 
@@ -493,46 +533,19 @@
     for j in range(1, n_lev):
         z_make(j).start()
 
-    rs_send(1, 4, 0, False)
-    rs_send(0, 4, 1, False)
-
-    rb_arrive()
-
-    def add_taps(j, acc):
-        return acc + rsr[j].astype(F32)
-
-    wown[...] = lax.fori_loop(1, n_chip, add_taps, dw[1, chip]) * (1.0 / total_cells)
-    w_copy = pltpu.make_async_copy(wown, gw_out.at[core, chip], out_sem.at[0])
-    w_copy.start()
-
-    def ab_make(j):
-        k = wrap(chip + j, n_chip)
-        return remote(wown, gw_out.at[core, chip], ab_ss.at[j], ab_rs.at[j], at_chip(k))
-
-    ab_arrive, ab_sent = over_chips(ab_make)
-    rs_send(0, 4, 0, False)
-    rs_send(1, 4, 1, False)
-
-    for j in range(1, n_lev):
-        z_make(j).wait_recv()
-    whole = extz[0]
-    for k in range(1, n_lev):
-        whole = whole + extz[k]
-    eown[...] = whole * (1.0 / total_cells)
-    e_copy = pltpu.make_async_copy(eown, ext_out.at[core, chip], out_sem.at[1])
-    e_copy.start()
-
-    def ac_make(j):
-        k = wrap(chip + j, n_chip)
-        return remote(eown, ext_out.at[core, chip], ac_ss.at[j], ac_rs.at[j], at_chip(k))
-
-    ac_arrive, ac_sent = over_chips(ac_make)
-
     for way, h in ((1, 0), (0, 1), (0, 0), (1, 1)):
         for k in range(cuts):
             rs_copies[way, far, h, k].wait_recv()
     g = jnp.concatenate(
-        [gu[2 * lev + h] + (arecv[0, far, h] + arecv[1, far, h]) for h in range(2)], axis=1
+        [
+            gu[2 * lev + h]
+            + jnp.concatenate(
+                [unpack(arecv[0, far, h, k]) + unpack(arecv[1, far, h, k]) for k in range(cuts)],
+                axis=0,
+            )
+            for h in range(2)
+        ],
+        axis=1,
     )
     at = lanes(2 * lev, 2)
     m_hi, m_lo = split(g * hr_s[:, at])
@@ -568,9 +581,20 @@
 
     ag_send(1)
     put(0, lev)
-    ac_arrive()
-    e_copy.wait()
-    pc = go(remote(ext_out.at[core], ext_out.at[core], pc_ss, pc_rs, pair))
+    for j in range(1, n_lev):
+        z_make(j).wait_recv()
+    whole = extz[0]
+    for k in range(1, n_lev):
+        whole = whole + extz[k]
+    eown[...] = whole * (1.0 / total_cells)
+    e_copy = pltpu.make_async_copy(eown, ext_out.at[core, chip], out_sem.at[1])
+    e_copy.start()
+
+    def ac_make(j):
+        k = wrap(chip + j, n_chip)
+        return remote(eown, ext_out.at[core, chip], ac_ss.at[j], ac_rs.at[j], at_chip(k))
+
+    ac_arrive, ac_sent = over_chips(ac_make)
     ag_send(2)
     put(1, wrap(lev + 1, n_lev))
     put(2, wrap(lev - 1, n_lev))
@@ -580,6 +604,9 @@
     ag_send(3)
     put(3, wrap(lev + 2, n_lev))
     put(4, wrap(lev - 2, n_lev))
+    ac_arrive()
+    e_copy.wait()
+    pc = go(remote(ext_out.at[core], ext_out.at[core], pc_ss, pc_rs, pair))
     ag_send(4)
     for way in range(2):
         for k in range(cuts):
@@ -697,7 +724,8 @@
         V((nn, wide), F32), V((nn // 2, wide), F32), V((n_chip, share, wide), F32),
         V((n_chip, share, wide), F32), V((n_lev, share, wide), F32),
         V((share, wide), F32),
-        V((2, far + 1, 2, nn, cols), F32), V((2, far + 1, 2, nn, cols), F32),
+        V((2, far + 1, 2, 2, nn // 4 * 3, cols), BF16),
+        V((2, far + 1, 2, 2, nn // 4 * 3, cols), BF16),
         V((rows, nn, cols), BF16),
         D((4,)), D((2,)), D((n_lev,)),
         D((2,)), D((2,)), D((6,)), D((6,)), D((2,)), D((2,)), D((6,)), D((6,)),

time: 83 us -> 77.4 us (0.933)
  Pallas kernels: 81.2 us -> 75.9 us
    pallas_call x1, Pallas kernels: 76.6 us -> 71.3 us  [local(): pl.pallas_call(functools.partial(kernel, dims), out_shape=(jax.ShapeDtype...]
where the time goes in v4:
time: 77.4 us; the launch traced here: 76.6 us
  Pallas kernels  75.9 us (98%)
    pallas_call x1, Pallas kernels, local(): pl.pallas_call(functools.partial(kernel, dims), out_shape=(jax.ShapeDtype...  71.3 us
    pallas_call x1, Pallas kernels, local(): pl.pallas_call(functools.partial(finish, (nn, rows, parts)), out_shape=(j...  4.63 us

profile of v4, /device:TPU:6, one launch (start us, length us, event | category | flops | bytes accessed | tf_op | source)
XLA Modules:
  0.0 76.6 jit_solution(5635848209357397442)
XLA Ops:
  0.6 71.3 %shard_map.110 = (bf16[16,256,128]{2,1,0:T(8,128)(2,1)}, f32[2,16,48,256]{3,2,1,0:T(8,128)}, f32[2,16,8,384]{3,2,1,0:T(8,128)}, f32[1,96]{1,0:T(1,128)}) custom-call(f32[128]{0:T(128)} %constant.2.clone.area_ref, bf16[256,16,128]{2,1,0:T(8,128)(2,1)} %hidden_ref.1, bf16[4,96,16,128]{3,2,1,0:T(8,128)(2,1)} %target_ref.1, bf16[16,96,256]{2,1,0:T(8,128)(2,1)} %weight_ref.1, ...), custom_call_target="tpu_custom_call" | custom-call | tf_op jit(solution)/shard_map/pallas_call | solution.py:741
  71.9 4.6 %shard_map.111 = (f32[4096,128]{1,0:T(8,128)}, f32[2,16,48,256]{3,2,1,0:T(8,128)}, f32[256,256]{1,0:T(8,128)}, f32[1,256]{1,0:T(1,128)}, f32[1,96]{1,0:T(1,128)}) custom-call(bf16[16,256,128]{2,1,0:T(8,128)(2,1)} %get-tuple-element.14.agr_ref, f32[2,16,48,256]{3,2,1,0:T(8,128)} %get-tuple-element.15.wg_ref, f32[2,16,8,384]{3,2,1,0:T(8,128)} %get-tuple-element.16.ext_ref, ...), custom_call_target="tpu_custom_call" | custom-call | tf_op jit(solution)/shard_map/pallas_call | solution.py:760

commit v5 on v4

--- a/solution.py
+++ b/solution.py
@@ -373,7 +373,14 @@
             ).astype(BF16)
         return c
 
-    lax.fori_loop(0, rows + 1, shift_g, 0)
+    def shift_pair(i, c):
+        shift_g(2 * i, c)
+        return shift_g(2 * i + 1, c)
+
+    far = n_lev // 2
+    opposite = wrap(lev + far, n_lev)
+    for r in range(3):
+        shift_g(2 * opposite + r, 0)
 
     def grad_rows(*chunks):
         moved = jnp.concatenate(
@@ -389,7 +396,6 @@
             gu[2 * k] = y[:, 2 * i * LANES : (2 * i + 1) * LANES]
             gu[2 * k + 1] = y[:, (2 * i + 1) * LANES : (2 * i + 2) * LANES]
 
-    far = n_lev // 2
     cuts = 2
     piece = nn // cuts
     rs_copies = {}
@@ -427,9 +433,11 @@
             lambda: lax.fori_loop(1, n_chip, sent, 0),
         )
 
-    grad_rows(wrap(lev + far, n_lev))
+    grad_rows(opposite)
     rs_send(0, 1, 0, True)
     rs_send(1, 1, 1, True)
+    lax.fori_loop(0, (rows + 1) // 2, shift_pair, 0)
+    shift_g(rows, 0)
     grad_rows(wrap(lev + far - 1, n_lev), wrap(lev + far + 1, n_lev))
     rs_send(1, 2, 0, True)
     rs_send(0, 2, 1, True)
@@ -672,6 +680,9 @@
                 i, k * step : (k + 1) * step, :
             ].astype(F32)
         store(k).start()
+        if k < 2:
+            fetch_gw(k).wait()
+            store_gw(k).start()
     fetch_ext.wait()
     full = ext_v[...].reshape(nn, nn + LANES)
     gg_v[...] = full[:, :nn]
@@ -679,9 +690,6 @@
     gbeta_out[...] = jnp.sum(
         jnp.where(eye, full[:, nn + LANES - 1 : nn + LANES], 0.0), axis=0, keepdims=True
     )
-    for k in range(2):
-        fetch_gw(k).wait()
-        store_gw(k).start()
     for k in range(parts):
         store(k).wait()
     store_gg.wait()

time: 77.4 us -> 77.6 us (level)
  no operation moved by 1% of the time
where the time goes in v5:
time: 77.6 us; the launch traced here: 76.7 us
  Pallas kernels  76.1 us (98%)
    pallas_call x1, Pallas kernels, local(): pl.pallas_call(functools.partial(kernel, dims), out_shape=(jax.ShapeDtype...  71.6 us
    pallas_call x1, Pallas kernels, local(): pl.pallas_call(functools.partial(finish, (nn, rows, parts)), out_shape=(j...  4.48 us

profile of v5, /device:TPU:6, one launch (start us, length us, event | category | flops | bytes accessed | tf_op | source)
XLA Modules:
  0.0 76.7 jit_solution(14011763616590278921)
XLA Ops:
  0.6 71.6 %shard_map.110 = (bf16[16,256,128]{2,1,0:T(8,128)(2,1)}, f32[2,16,48,256]{3,2,1,0:T(8,128)}, f32[2,16,8,384]{3,2,1,0:T(8,128)}, f32[1,96]{1,0:T(1,128)}) custom-call(f32[128]{0:T(128)} %constant.2.clone.area_ref, bf16[256,16,128]{2,1,0:T(8,128)(2,1)} %hidden_ref.1, bf16[4,96,16,128]{3,2,1,0:T(8,128)(2,1)} %target_ref.1, bf16[16,96,256]{2,1,0:T(8,128)(2,1)} %weight_ref.1, ...), custom_call_target="tpu_custom_call" | custom-call | tf_op jit(solution)/shard_map/pallas_call | solution.py:749
  72.2 4.5 %shard_map.111 = (f32[4096,128]{1,0:T(8,128)}, f32[2,16,48,256]{3,2,1,0:T(8,128)}, f32[256,256]{1,0:T(8,128)}, f32[1,256]{1,0:T(1,128)}, f32[1,96]{1,0:T(1,128)}) custom-call(bf16[16,256,128]{2,1,0:T(8,128)(2,1)} %get-tuple-element.14.agr_ref, f32[2,16,48,256]{3,2,1,0:T(8,128)} %get-tuple-element.15.wg_ref, f32[2,16,8,384]{3,2,1,0:T(8,128)} %get-tuple-element.16.ext_ref, ...), custom_call_target="tpu_custom_call" | custom-call | tf_op jit(solution)/shard_map/pallas_call | solution.py:768

commit v6 on v5

--- a/solution.py
+++ b/solution.py
@@ -59,8 +59,8 @@
     hid_v, tgt_v, w_v, gamma_v,
     hf, tf, hx, root_s, hr_s, sqh, sql, g3, gt3, wt,
     us, gs, sel, hh_send, hh_recv, eu_send, eu_recv, eg_send, eg_recv, eg_corner,
-    dw, dwp, rsb, rsr, wown,
-    gu, bacc, mh, ml, ext, extp, exts, extr, extz, eown,
+    dw, dwp, rsb, rsr, wg,
+    gu, bacc, mh, ml, ext, extp, exts, extr, extz, extg,
     abuf, arecv, agr,
     in_sem, out_sem, put_sem,
     row_ss, row_rs, eu_ss, eu_rs, grow_ss, grow_rs, eg_ss, eg_rs,
@@ -512,13 +512,12 @@
     def add_taps(j, acc):
         return acc + rsr[j].astype(F32)
 
-    wown[...] = lax.fori_loop(1, n_chip, add_taps, dw[1, chip]) * (1.0 / total_cells)
-    w_copy = pltpu.make_async_copy(wown, gw_out.at[core, chip], out_sem.at[0])
-    w_copy.start()
+    wg[core, chip] = lax.fori_loop(1, n_chip, add_taps, dw[1, chip]) * (1.0 / total_cells)
 
     def ab_make(j):
         k = wrap(chip + j, n_chip)
-        return remote(wown, gw_out.at[core, chip], ab_ss.at[j], ab_rs.at[j], at_chip(k))
+        block = wg.at[core, chip]
+        return remote(block, block, ab_ss.at[j], ab_rs.at[j], at_chip(k))
 
     ab_arrive, ab_sent = over_chips(ab_make)
     rs_send(0, 4, 0, False)
@@ -594,35 +593,40 @@
     whole = extz[0]
     for k in range(1, n_lev):
         whole = whole + extz[k]
-    eown[...] = whole * (1.0 / total_cells)
-    e_copy = pltpu.make_async_copy(eown, ext_out.at[core, chip], out_sem.at[1])
-    e_copy.start()
+    extg[core, chip] = whole * (1.0 / total_cells)
 
     def ac_make(j):
         k = wrap(chip + j, n_chip)
-        return remote(eown, ext_out.at[core, chip], ac_ss.at[j], ac_rs.at[j], at_chip(k))
+        block = extg.at[core, chip]
+        return remote(block, block, ac_ss.at[j], ac_rs.at[j], at_chip(k))
 
     ac_arrive, ac_sent = over_chips(ac_make)
     ag_send(2)
     put(1, wrap(lev + 1, n_lev))
     put(2, wrap(lev - 1, n_lev))
     ab_arrive()
-    w_copy.wait()
-    pg = go(remote(gw_out.at[core], gw_out.at[core], pg_ss, pg_rs, pair))
+    pg = go(remote(wg.at[core], wg.at[core], pg_ss, pg_rs, pair))
+    w_copies = [
+        pltpu.make_async_copy(wg.at[part], gw_out.at[part], out_sem.at[i])
+        for i, part in enumerate((core, 1 - core))
+    ]
+    w_copies[0].start()
     ag_send(3)
     put(3, wrap(lev + 2, n_lev))
     put(4, wrap(lev - 2, n_lev))
     ac_arrive()
-    e_copy.wait()
-    pc = go(remote(ext_out.at[core], ext_out.at[core], pc_ss, pc_rs, pair))
+    pc = go(remote(extg.at[core], extg.at[core], pc_ss, pc_rs, pair))
     ag_send(4)
     for way in range(2):
         for k in range(cuts):
             ag_copies[way, far - 1, 1 - way, k].wait_recv()
     put(5, wrap(lev + 3, n_lev))
     put(6, wrap(lev - 3, n_lev))
+    pg.wait_recv()
+    w_copies[1].start()
     pc.wait_recv()
-    pg.wait_recv()
+    e_copy = pltpu.make_async_copy(extg, ext_out, out_sem.at[2])
+    e_copy.start()
     for way in range(2):
         for k in range(cuts):
             ag_copies[way, far, way, k].wait_recv()
@@ -636,7 +640,7 @@
     ac_sent()
     for j in range(1, n_lev):
         z_make(j).wait_send()
-    for c in put_copies:
+    for c in put_copies + w_copies + [e_copy]:
         c.wait()
 
 
@@ -727,15 +731,15 @@
         V((2, 32, nn), BF16), V((6, 32, nn), BF16),
         V((2, 2, 32, cols), BF16), V((2, 2, 32, cols), BF16), V((2, 2, 32, cols), BF16),
         V((2, n_chip, half, nn), F32), V((n_chip, half, nn), F32), V((n_chip, half, nn), BF16),
-        V((n_chip, half, nn), BF16), V((half, nn), F32),
+        V((n_chip, half, nn), BF16), V((2, n_chip, half, nn), F32),
         V((rows, nn, cols), F32), V((cols, cols), F32), V((nn, cells), BF16), V((nn, cells), BF16),
         V((nn, wide), F32), V((nn // 2, wide), F32), V((n_chip, share, wide), F32),
         V((n_chip, share, wide), F32), V((n_lev, share, wide), F32),
-        V((share, wide), F32),
+        V((2, n_chip, share, wide), F32),
         V((2, far + 1, 2, 2, nn // 4 * 3, cols), BF16),
         V((2, far + 1, 2, 2, nn // 4 * 3, cols), BF16),
         V((rows, nn, cols), BF16),
-        D((4,)), D((2,)), D((n_lev,)),
+        D((4,)), D((3,)), D((n_lev,)),
         D((2,)), D((2,)), D((6,)), D((6,)), D((2,)), D((2,)), D((6,)), D((6,)),
         D, D, D((n_chip,)), D((n_chip,)), D((n_chip,)), D((n_chip,)), D, D,
         D, D, D((n_chip,)), D((n_chip,)), D((n_lev,)), D((n_lev,)), D((n_chip,)), D((n_chip,)),

time: 77.6 us -> 77.5 us (level)
  no operation moved by 1% of the time
where the time goes in v6:
time: 77.5 us; the launch traced here: 76.6 us
  Pallas kernels  76 us (98%)
    pallas_call x1, Pallas kernels, local(): pl.pallas_call(functools.partial(kernel, dims), out_shape=(jax.ShapeDtype...  71.5 us
    pallas_call x1, Pallas kernels, local(): pl.pallas_call(functools.partial(finish, (nn, rows, parts)), out_shape=(j...  4.48 us

profile of v6, /device:TPU:6, one launch (start us, length us, event | category | flops | bytes accessed | tf_op | source)
XLA Modules:
  0.0 76.6 jit_solution(8782718505246240864)
XLA Ops:
  0.6 71.5 %shard_map.110 = (bf16[16,256,128]{2,1,0:T(8,128)(2,1)}, f32[2,16,48,256]{3,2,1,0:T(8,128)}, f32[2,16,8,384]{3,2,1,0:T(8,128)}, f32[1,96]{1,0:T(1,128)}) custom-call(f32[128]{0:T(128)} %constant.2.clone.area_ref, bf16[256,16,128]{2,1,0:T(8,128)(2,1)} %hidden_ref.1, bf16[4,96,16,128]{3,2,1,0:T(8,128)(2,1)} %target_ref.1, bf16[16,96,256]{2,1,0:T(8,128)(2,1)} %weight_ref.1, ...), custom_call_target="tpu_custom_call" | custom-call | tf_op jit(solution)/shard_map/pallas_call | solution.py:753
  72.1 4.5 %shard_map.111 = (f32[4096,128]{1,0:T(8,128)}, f32[2,16,48,256]{3,2,1,0:T(8,128)}, f32[256,256]{1,0:T(8,128)}, f32[1,256]{1,0:T(1,128)}, f32[1,96]{1,0:T(1,128)}) custom-call(bf16[16,256,128]{2,1,0:T(8,128)(2,1)} %get-tuple-element.14.agr_ref, f32[2,16,48,256]{3,2,1,0:T(8,128)} %get-tuple-element.15.wg_ref, f32[2,16,8,384]{3,2,1,0:T(8,128)} %get-tuple-element.16.ext_ref, ...), custom_call_target="tpu_custom_call" | custom-call | tf_op jit(solution)/shard_map/pallas_call | solution.py:772

commit v7 on v6

--- a/solution.py
+++ b/solution.py
@@ -456,6 +456,8 @@
         return remote(rsb.at[k], rsr.at[j], rb_ss.at[j], rb_rs.at[j], at_chip(k))
 
     rb_arrive, rb_sent = over_chips(rb_make)
+    rs_send(0, 2, 0, False)
+    rs_send(1, 2, 1, False)
     grad_rows(wrap(lev + far - 2, n_lev), wrap(lev + far + 2, n_lev))
     grad_rows(wrap(lev + 1, n_lev), wrap(lev + n_lev - 1, n_lev))
     grad_rows(lev)
@@ -480,9 +482,6 @@
     mine = pl.multiple_of(core * (nn // 2), nn // 2)
     others = pl.multiple_of((1 - core) * (nn // 2), nn // 2)
     pe = go(remote(ext.at[pl.ds(others, nn // 2)], extp, pe_ss, pe_rs, pair))
-
-    rs_send(0, 2, 0, False)
-    rs_send(1, 2, 1, False)
 
     pe.wait_recv()
 

time: 77.5 us -> 76.7 us (0.990)
  no operation moved by 1% of the time
where the time goes in v7:
time: 76.7 us; the launch traced here: 76.2 us
  Pallas kernels  75.5 us (98%)
    pallas_call x1, Pallas kernels, local(): pl.pallas_call(functools.partial(kernel, dims), out_shape=(jax.ShapeDtype...  71.1 us
    pallas_call x1, Pallas kernels, local(): pl.pallas_call(functools.partial(finish, (nn, rows, parts)), out_shape=(j...  4.48 us

profile of v7, /device:TPU:6, one launch (start us, length us, event | category | flops | bytes accessed | tf_op | source)
XLA Modules:
  0.0 76.2 jit_solution(15526931141134047337)
XLA Ops:
  0.6 71.1 %shard_map.110 = (bf16[16,256,128]{2,1,0:T(8,128)(2,1)}, f32[2,16,48,256]{3,2,1,0:T(8,128)}, f32[2,16,8,384]{3,2,1,0:T(8,128)}, f32[1,96]{1,0:T(1,128)}) custom-call(f32[128]{0:T(128)} %constant.2.clone.area_ref, bf16[256,16,128]{2,1,0:T(8,128)(2,1)} %hidden_ref.1, bf16[4,96,16,128]{3,2,1,0:T(8,128)(2,1)} %target_ref.1, bf16[16,96,256]{2,1,0:T(8,128)(2,1)} %weight_ref.1, ...), custom_call_target="tpu_custom_call" | custom-call | tf_op jit(solution)/shard_map/pallas_call | solution.py:752
  71.7 4.5 %shard_map.111 = (f32[4096,128]{1,0:T(8,128)}, f32[2,16,48,256]{3,2,1,0:T(8,128)}, f32[256,256]{1,0:T(8,128)}, f32[1,256]{1,0:T(1,128)}, f32[1,96]{1,0:T(1,128)}) custom-call(bf16[16,256,128]{2,1,0:T(8,128)(2,1)} %get-tuple-element.14.agr_ref, f32[2,16,48,256]{3,2,1,0:T(8,128)} %get-tuple-element.15.wg_ref, f32[2,16,8,384]{3,2,1,0:T(8,128)} %get-tuple-element.16.ext_ref, ...), custom_call_target="tpu_custom_call" | custom-call | tf_op jit(solution)/shard_map/pallas_call | solution.py:771
